TPU v7x, 256 devices: a whole 4x4x8 slice. The times are simulated.
256 devices in a mesh: ctx: 8 (over y_lo, x), zero: 32 (over z, y_hi, core).
Axes of the slice: x: 4, y: 4 (y_hi: 2, y_lo: 2; y = y_hi * 2 + y_lo), z: 8, core: 2. Of those that a mesh axis runs over, the one named last changes fastest.
Arguments:
- tokens: bfloat16 [4, 2048, 8192], P(None, 'ctx', 'zero'), may hold values from -48 to 48
- q_weight: bfloat16 [8192, 4096], P('zero'), may hold values from -0.0625 to 0.0625
- forget_weight: bfloat16 [8192, 4096], P('zero'), may hold values from -0.0625 to 0.0625
- value_weight: bfloat16 [8192, 4096], P('zero'), may hold values from -0.0625 to 0.0625
- forget_bias: float32 [4096], P('zero'), may hold values from 3 to 16
- norm_gain: float32 [4096], P('zero'), may hold values from 0.1 to 1.9
Outputs:
- head_out: bfloat16 [4, 2048, 4096], P(None, 'ctx', 'zero')
All inputs are finite; a program needn't handle non-finite values.
Results may differ from a plain program's by a relative error of at most 0.0015.
Values may be sent and summed in bfloat16 or wider, within the bound.
A program may use at most 128 MiB of HBM per device.

v0:
```python
import jax
import jax.numpy as jnp
from jax import lax
from jax.sharding import PartitionSpec as P

HEAD = 128
BLK = 64


def from_behind(value, axis, steps):
    count = lax.axis_size(axis)
    first, last = (max(0, -steps), min(count, count - steps))
    return lax.ppermute(value, axis, [(source, source + steps) for source in range(first, last)])


def block_step(carried, block):
    queries, log_forget, in_gate, values = block
    cum_log = jnp.cumsum(log_forget, axis=0)
    log_gap = cum_log[:, None, :] - cum_log[None, :, :]
    positions = jnp.arange(queries.shape[0], dtype=jnp.int32)
    causal = (positions[:, None] >= positions[None, :])[:, :, None]
    decays = jnp.where(causal, jnp.exp(jnp.minimum(log_gap, 0.0)), 0.0)
    scores = jnp.einsum("tc,sc,tsc->ts", queries, in_gate, decays, precision=lax.Precision.HIGHEST)
    within = jnp.dot(scores, values, precision=lax.Precision.HIGHEST)
    from_state = jnp.dot(queries * jnp.exp(cum_log), carried, precision=lax.Precision.HIGHEST)
    to_end = jnp.exp(cum_log[-1:] - cum_log)
    updated = jnp.exp(cum_log[-1])[:, None] * carried + jnp.dot(
        (in_gate * to_end).T, values, precision=lax.Precision.HIGHEST
    )
    return (updated, within + from_state)


def scan_blocks(queries, log_forget, in_gate, values):
    block_count = queries.shape[0] // BLK
    shaped = tuple(
        (
            item.reshape(block_count, BLK, item.shape[1])
            for item in (queries, log_forget, in_gate, values)
        )
    )
    start_state = jnp.zeros((queries.shape[1], values.shape[1]), jnp.float32)
    final_state, outputs = lax.scan(block_step, start_state, shaped)
    return (outputs.reshape(queries.shape), final_state)


def body(tokens, q_weight, forget_weight, value_weight, forget_bias, norm_gain):
    seq_count, tok_rows = (tokens.shape[0], tokens.shape[1])
    q_cols = lax.all_to_all(q_weight, "zero", split_axis=1, concat_axis=0, tiled=True)
    forget_cols = lax.all_to_all(forget_weight, "zero", split_axis=1, concat_axis=0, tiled=True)
    value_cols = lax.all_to_all(value_weight, "zero", split_axis=1, concat_axis=0, tiled=True)
    local_width = q_cols.shape[1]
    heads_here = local_width // HEAD
    piece = lax.all_gather(tokens, "zero", axis=2, tiled=True)
    results = []
    for index, matrix in enumerate((q_cols, forget_cols, value_cols)):
        results.append(jnp.einsum("stc,ch->sth", piece, matrix, preferred_element_type=jnp.float32))
    queries, logit, values = tuple(results)
    logit = logit + forget_bias
    log_forget = jax.nn.log_sigmoid(logit)
    in_gate = jax.nn.sigmoid(-logit)

    def by_head(item):
        return (
            item.reshape(seq_count, tok_rows, heads_here, HEAD)
            .transpose(0, 2, 1, 3)
            .reshape(seq_count * heads_here, tok_rows, HEAD)
        )

    queries, log_forget, in_gate, values = (
        by_head(queries),
        by_head(log_forget),
        by_head(in_gate),
        by_head(values),
    )
    local_out, own_state = jax.vmap(scan_blocks)(queries, log_forget, in_gate, values)
    cum_log = jnp.cumsum(log_forget, axis=1)
    total_log = cum_log[:, -1]
    incoming = jnp.zeros_like(own_state)
    for turn_index in range(lax.axis_size("ctx") - 1):
        incoming = from_behind(jnp.exp(total_log)[:, :, None] * incoming + own_state, "ctx", 1)
    outputs = local_out + jnp.einsum(
        "btc,bcv->btv", queries * jnp.exp(cum_log), incoming, precision=lax.Precision.HIGHEST
    )
    mean_square = jnp.mean(outputs * outputs, axis=-1, keepdims=True)
    outputs = outputs.reshape(seq_count, heads_here, tok_rows, HEAD)
    mean_square = mean_square.reshape(seq_count, heads_here, tok_rows, 1)
    gains = norm_gain.reshape(heads_here, HEAD)[None, :, None, :]
    normed = (outputs * lax.rsqrt(mean_square + 1e-05) * gains).astype(jnp.bfloat16)
    return normed.transpose(0, 2, 1, 3).reshape(seq_count, tok_rows, local_width)


def solution(mesh):
    placed = (
        P(None, "ctx", "zero"),
        P("zero", None),
        P("zero", None),
        P("zero", None),
        P("zero"),
        P("zero"),
    )
    return jax.shard_map(
        body, mesh=mesh, in_specs=placed, out_specs=P(None, "ctx", "zero"), check_vma=False
    )
```

profile of v0, /device:TPU:24, one launch (start us, length us, event | category | flops | bytes accessed | tf_op | source)
XLA Modules:
  0.0 431.7 jit_solution(1455316876139064295)
XLA Ops:
  8.1 1.9 copy_bitcast_fusion.2
  10.0 11.6 %all-to-all-start = ((bf16[256,32,128]{2,0,1:T(8,128)(2,1)}), bf16[256,32,128]{2,0,1:T(8,128)(2,1)}, u32[]{:S(2)}, u32[]{:S(2)}) async-start(bf16[256,32,128]{2,0,1:T(8,128)(2,1)} %copy_bitcast_fusion.2), calls=%async_computation | async-start | bytes 4194304 | tf_op jit(solution)/shard_map/all_to_all | solution.py:49
  21.7 3.5 copy_bitcast_fusion
  25.2 60.9 %all-to-all-done = bf16[256,32,128]{2,0,1:T(8,128)(2,1)} async-done(((bf16[256,32,128]{2,0,1:T(8,128)(2,1)}), bf16[256,32,128]{2,0,1:T(8,128)(2,1)}, u32[]{:S(2)}, u32[]{:S(2)}) %all-to-all-start) | async-done | bytes 2097184 | tf_op jit(solution)/shard_map/all_to_all | solution.py:49
  86.1 5.0 %all-to-all-start.2 = ((bf16[256,32,128]{2,0,1:T(8,128)(2,1)}), bf16[256,32,128]{2,0,1:T(8,128)(2,1)}, u32[]{:S(2)}, u32[]{:S(2)}) async-start(bf16[256,32,128]{2,0,1:T(8,128)(2,1)} %copy_bitcast_fusion), calls=%async_computation.2 | async-start | bytes 4194304 | tf_op jit(solution)/shard_map/all_to_all | solution.py:48
  91.1 3.5 copy_bitcast_fusion.1
  94.6 58.6 %all-to-all-done.2 = bf16[256,32,128]{2,0,1:T(8,128)(2,1)} async-done(((bf16[256,32,128]{2,0,1:T(8,128)(2,1)}), bf16[256,32,128]{2,0,1:T(8,128)(2,1)}, u32[]{:S(2)}, u32[]{:S(2)}) %all-to-all-start.2) | async-done | bytes 2097184 | tf_op jit(solution)/shard_map/all_to_all | solution.py:48
  153.2 7.0 %all-to-all-start.1 = ((bf16[256,32,128]{2,0,1:T(8,128)(2,1)}), bf16[256,32,128]{2,0,1:T(8,128)(2,1)}, u32[]{:S(2)}, u32[]{:S(2)}) async-start(bf16[256,32,128]{2,0,1:T(8,128)(2,1)} %copy_bitcast_fusion.1), calls=%async_computation.1 | async-start | bytes 4194304 | tf_op jit(solution)/shard_map/all_to_all | solution.py:50
  160.3 89.1 %all-gather.2.cloned.1.call-done = bf16[4,256,8192]{2,1,0:T(8,128)(2,1)} async-done(((bf16[4,256,256]{2,1,0:T(8,128)(2,1)}), bf16[4,256,8192]{2,1,0:T(8,128)(2,1)}) %all-gather.2.cloned.1.call-update) | async-done | bytes 16777232 | tf_op jit(solution)/shard_map/all_gather | solution.py:53
  249.4 12.3 %add_divide_fusion = (f32[4,256,128]{2,1,0:T(8,128)S(1)}, f32[4,256,128]{2,1,0:T(8,128)S(1)}, f32[4,256,128]{2,1,0:T(8,128)}) fusion(f32[128]{0:T(128)S(1)} %copy-done.4, bf16[4,256,8192]{2,1,0:T(8,128)(2,1)} %all-gather.2.cloned.1.call-done, bf16[8192,128,1]{1,0,2:T(8,128)(2,1)} %bitcast.3), kind=kOutput, calls=%fused_computation.56 | convolution fusion | flops 2148925440 | bytes 20447744 | tf_op jit(solution)/shard_map/stc,ch->sth/dot_general | solution.py:56
  262.5 6.1 %fusion.31 = f32[4,256,128]{2,1,0:T(8,128)S(1)} fusion(bf16[4,256,8192]{2,1,0:T(8,128)(2,1)S(1)} %copy-done.3, bf16[8192,128,1]{1,0,2:T(8,128)(2,1)} %bitcast.16), kind=kOutput, calls=%fused_computation.69 | convolution fusion | flops 2147483648 | bytes 19398656 | tf_op jit(solution)/shard_map/stc,ch->sth/dot_general | solution.py:56
  270.3 11.6 %convolution_bitcast_fusion = f32[4,4,64,128]{3,2,0,1:T(8,128)} fusion(bf16[4,4,64,8192]{3,2,1,0:T(8,128)(2,1)} %bitcast.150, bf16[8192,128,1,1]{1,0,3,2:T(8,128)(2,1)} %bitcast.12), kind=kOutput, calls=%fused_computation.36 | convolution fusion | flops 2147483648 | bytes 19398656 | tf_op jit(solution)/shard_map/stc,ch->sth/dot_general | solution.py:56
  282.0 60.3 %while.13 = (s32[]{:T(128)}, f32[4,128,128]{2,1,0:T(8,128)S(1)}, f32[4,4,64,128]{3,2,0,1:T(8,128)}, f32[4,4,64,128]{3,2,1,0:T(8,128)}, f32[4,4,64,128]{3,2,1,0:T...) while((s32[]{:T(128)}, f32[4,128,128]{2,1,0:T(8,128)S(1)}, ...), condition=%wide.region_2.3_spmd.clone, body=%wide.region_0.2_spmd.clone.sunk | while | flops 140857344 | bytes 20339324 | solution.py:42
  285.7 7.4 %fusion.54 = f32[4,64,64]{1,2,0:T(8,128)S(1)} fusion(f32[4,64,64,128]{3,2,1,0:T(8,128)S(1)} %exponential_select_fusion.2, f32[4,128,64]{1,2,0:T(8,128)S(1)} %get-tuple-element.159, f32[4,128,64]{1,2,0:T(8,128)S(1)} %dynamic-slice_bitcast_fusion.6), kind=kLoop, calls=%fused_computation.1.clone.1 | loop fusion | flops 6275072 | bytes 8716288 | tf_op jit(solution)/shard_map/vmap()/while/body/eval_jaxpr/tc,sc,tsc->ts/dot_general | solution.py:23
  300.7 7.4 %fusion.54 = f32[4,64,64]{1,2,0:T(8,128)S(1)} fusion(f32[4,64,64,128]{3,2,1,0:T(8,128)S(1)} %exponential_select_fusion.2, f32[4,128,64]{1,2,0:T(8,128)S(1)} %get-tuple-element.159, f32[4,128,64]{1,2,0:T(8,128)S(1)} %dynamic-slice_bitcast_fusion.6), kind=kLoop, calls=%fused_computation.1.clone.1 | loop fusion | flops 6275072 | bytes 8716288 | tf_op jit(solution)/shard_map/vmap()/while/body/eval_jaxpr/tc,sc,tsc->ts/dot_general | solution.py:23
  315.8 7.4 %fusion.54 = f32[4,64,64]{1,2,0:T(8,128)S(1)} fusion(f32[4,64,64,128]{3,2,1,0:T(8,128)S(1)} %exponential_select_fusion.2, f32[4,128,64]{1,2,0:T(8,128)S(1)} %get-tuple-element.159, f32[4,128,64]{1,2,0:T(8,128)S(1)} %dynamic-slice_bitcast_fusion.6), kind=kLoop, calls=%fused_computation.1.clone.1 | loop fusion | flops 6275072 | bytes 8716288 | tf_op jit(solution)/shard_map/vmap()/while/body/eval_jaxpr/tc,sc,tsc->ts/dot_general | solution.py:23
  330.9 7.4 %fusion.54 = f32[4,64,64]{1,2,0:T(8,128)S(1)} fusion(f32[4,64,64,128]{3,2,1,0:T(8,128)S(1)} %exponential_select_fusion.2, f32[4,128,64]{1,2,0:T(8,128)S(1)} %get-tuple-element.159, f32[4,128,64]{1,2,0:T(8,128)S(1)} %dynamic-slice_bitcast_fusion.6), kind=kLoop, calls=%fused_computation.1.clone.1 | loop fusion | flops 6275072 | bytes 8716288 | tf_op jit(solution)/shard_map/vmap()/while/body/eval_jaxpr/tc,sc,tsc->ts/dot_general | solution.py:23
  344.6 3.4 collective-permute-start
  348.0 9.0 %collective-permute-done = f32[4,128,128]{1,2,0:T(8,128)S(1)} collective-permute-done((f32[4,128,128]{1,2,0:T(8,128)S(1)}, f32[4,128,128]{1,2,0:T(8,128)S(1)}, u32[]{:S(2)}, u32[]{:S(2)}) %collective-permute-start) | collective-permute-done | bytes 262176 | tf_op jit(solution)/shard_map/ppermute | solution.py:13
  357.1 1.9 collective-permute-start.1
  359.0 9.7 %collective-permute-done.1 = f32[4,128,128]{1,2,0:T(8,128)S(1)} collective-permute-done((f32[4,128,128]{1,2,0:T(8,128)S(1)}, f32[4,128,128]{1,2,0:T(8,128)S(1)}, u32[]{:S(2)}, u32[]{:S(2)}) %collective-permute-start.1) | collective-permute-done | bytes 262176 | tf_op jit(solution)/shard_map/ppermute | solution.py:13
  368.8 1.9 collective-permute-start.2
  370.7 8.8 %collective-permute-done.2 = f32[4,128,128]{1,2,0:T(8,128)S(1)} collective-permute-done((f32[4,128,128]{1,2,0:T(8,128)S(1)}, f32[4,128,128]{1,2,0:T(8,128)S(1)}, u32[]{:S(2)}, u32[]{:S(2)}) %collective-permute-start.2) | collective-permute-done | bytes 262176 | tf_op jit(solution)/shard_map/ppermute | solution.py:13
  379.6 1.9 collective-permute-start.3
  381.5 8.4 %collective-permute-done.3 = f32[4,128,128]{1,2,0:T(8,128)S(1)} collective-permute-done((f32[4,128,128]{1,2,0:T(8,128)S(1)}, f32[4,128,128]{1,2,0:T(8,128)S(1)}, u32[]{:S(2)}, u32[]{:S(2)}) %collective-permute-start.3) | collective-permute-done | bytes 262176 | tf_op jit(solution)/shard_map/ppermute | solution.py:13
  390.0 1.9 collective-permute-start.4
  391.9 8.4 %collective-permute-done.4 = f32[4,128,128]{1,2,0:T(8,128)S(1)} collective-permute-done((f32[4,128,128]{1,2,0:T(8,128)S(1)}, f32[4,128,128]{1,2,0:T(8,128)S(1)}, u32[]{:S(2)}, u32[]{:S(2)}) %collective-permute-start.4) | collective-permute-done | bytes 262176 | tf_op jit(solution)/shard_map/ppermute | solution.py:13
  400.4 1.9 collective-permute-start.5
  402.3 8.4 %collective-permute-done.5 = f32[4,128,128]{1,2,0:T(8,128)S(1)} collective-permute-done((f32[4,128,128]{1,2,0:T(8,128)S(1)}, f32[4,128,128]{1,2,0:T(8,128)S(1)}, u32[]{:S(2)}, u32[]{:S(2)}) %collective-permute-start.5) | collective-permute-done | bytes 262176 | tf_op jit(solution)/shard_map/ppermute | solution.py:13
  411.5 1.9 collective-permute-start.6
  414.7 7.4 %collective-permute-done.6 = f32[4,128,128]{1,2,0:T(8,128)S(1)} collective-permute-done((f32[4,128,128]{1,2,0:T(8,128)}, f32[4,128,128]{1,2,0:T(8,128)S(1)}, u32[]{:S(2)}, u32[]{:S(2)}) %collective-permute-start.6) | collective-permute-done | bytes 262176 | tf_op jit(solution)/shard_map/ppermute | solution.py:13
  422.1 1.8 multiply_reduce_fusion
  (78 shorter events, 40.1 us)
Async XLA Ops:
  6.5 1.6 copy-start
  6.5 242.9 %all-gather.2.cloned.1.call-start = ((), (), s32[]{:S(2)}) async-start(), calls=%async_computation.3 | async-start | bytes 17301504 | tf_op jit(solution)/shard_map/all_gather | solution.py:53
  10.0 76.0 %all-to-all-start = ((bf16[256,32,128]{2,0,1:T(8,128)(2,1)}), bf16[256,32,128]{2,0,1:T(8,128)(2,1)}, u32[]{:S(2)}, u32[]{:S(2)}) async-start(bf16[256,32,128]{2,0,1:T(8,128)(2,1)} %copy_bitcast_fusion.2), calls=%async_computation | async-start | bytes 4194304 | tf_op jit(solution)/shard_map/all_to_all | solution.py:49
  86.1 67.1 %all-to-all-start.2 = ((bf16[256,32,128]{2,0,1:T(8,128)(2,1)}), bf16[256,32,128]{2,0,1:T(8,128)(2,1)}, u32[]{:S(2)}, u32[]{:S(2)}) async-start(bf16[256,32,128]{2,0,1:T(8,128)(2,1)} %copy_bitcast_fusion), calls=%async_computation.2 | async-start | bytes 4194304 | tf_op jit(solution)/shard_map/all_to_all | solution.py:48
  94.6 154.8 %copy-start.4 = (f32[128]{0:T(128)S(1)}, f32[128]{0:T(128)}, u32[]{:S(2)}) copy-start(f32[128]{0:T(128)} %param.12) | copy-start | bytes 1540
  153.2 117.1 %all-to-all-start.1 = ((bf16[256,32,128]{2,0,1:T(8,128)(2,1)}), bf16[256,32,128]{2,0,1:T(8,128)(2,1)}, u32[]{:S(2)}, u32[]{:S(2)}) async-start(bf16[256,32,128]{2,0,1:T(8,128)(2,1)} %copy_bitcast_fusion.1), calls=%async_computation.1 | async-start | bytes 4194304 | tf_op jit(solution)/shard_map/all_to_all | solution.py:50
  249.4 13.1 %copy-start.3 = (bf16[4,256,8192]{2,1,0:T(8,128)(2,1)S(1)}, bf16[4,256,8192]{2,1,0:T(8,128)(2,1)}, u32[]{:S(2)}) copy-start(bf16[4,256,8192]{2,1,0:T(8,128)(2,1)} %all-gather.2.cloned.1.call-done) | copy-start | bytes 50331652
  268.6 0.8 copy-start.1
  344.6 12.5 %collective-permute-start = (f32[4,128,128]{1,2,0:T(8,128)S(1)}, f32[4,128,128]{1,2,0:T(8,128)S(1)}, u32[]{:S(2)}, u32[]{:S(2)}) collective-permute-start(f32[4,128,128]{1,2,0:T(8,128)S(1)} %broadcast_add_fusion.1), channel_id=1, source_target_pairs={{0,32},{32,64},{64,96},{96,128},{128,160},{160,192},{192,224},{1,3... | collective-permute-start | bytes 786440 | tf_op jit(solution)/shard_map/ppermute | solution.py:13
  357.1 11.7 %collective-permute-start.1 = (f32[4,128,128]{1,2,0:T(8,128)S(1)}, f32[4,128,128]{1,2,0:T(8,128)S(1)}, u32[]{:S(2)}, u32[]{:S(2)}) collective-permute-start(f32[4,128,128]{1,2,0:T(8,128)S(1)} %multiply_add_fusion.5), channel_id=1, source_target_pairs={{0,32},{32,64},{64,96},{96,128},{128,160},{160,192},{192,224},{1,3... | collective-permute-start | bytes 786440 | tf_op jit(solution)/shard_map/ppermute | solution.py:13
  368.8 10.7 %collective-permute-start.2 = (f32[4,128,128]{1,2,0:T(8,128)S(1)}, f32[4,128,128]{1,2,0:T(8,128)S(1)}, u32[]{:S(2)}, u32[]{:S(2)}) collective-permute-start(f32[4,128,128]{1,2,0:T(8,128)S(1)} %multiply_add_fusion.4), channel_id=1, source_target_pairs={{0,32},{32,64},{64,96},{96,128},{128,160},{160,192},{192,224},{1,3... | collective-permute-start | bytes 786440 | tf_op jit(solution)/shard_map/ppermute | solution.py:13
  379.6 10.4 %collective-permute-start.3 = (f32[4,128,128]{1,2,0:T(8,128)S(1)}, f32[4,128,128]{1,2,0:T(8,128)S(1)}, u32[]{:S(2)}, u32[]{:S(2)}) collective-permute-start(f32[4,128,128]{1,2,0:T(8,128)S(1)} %multiply_add_fusion.3), channel_id=1, source_target_pairs={{0,32},{32,64},{64,96},{96,128},{128,160},{160,192},{192,224},{1,3... | collective-permute-start | bytes 786440 | tf_op jit(solution)/shard_map/ppermute | solution.py:13
  390.0 10.4 %collective-permute-start.4 = (f32[4,128,128]{1,2,0:T(8,128)S(1)}, f32[4,128,128]{1,2,0:T(8,128)S(1)}, u32[]{:S(2)}, u32[]{:S(2)}) collective-permute-start(f32[4,128,128]{1,2,0:T(8,128)S(1)} %multiply_add_fusion.2), channel_id=1, source_target_pairs={{0,32},{32,64},{64,96},{96,128},{128,160},{160,192},{192,224},{1,3... | collective-permute-start | bytes 786440 | tf_op jit(solution)/shard_map/ppermute | solution.py:13
  400.4 23.5 %copy-start.2 = (f32[128]{0:T(128)S(1)}, f32[128]{0:T(128)}, u32[]{:S(2)}) copy-start(f32[128]{0:T(128)} %param.13) | copy-start | bytes 1540
  400.4 10.4 %collective-permute-start.5 = (f32[4,128,128]{1,2,0:T(8,128)S(1)}, f32[4,128,128]{1,2,0:T(8,128)S(1)}, u32[]{:S(2)}, u32[]{:S(2)}) collective-permute-start(f32[4,128,128]{1,2,0:T(8,128)S(1)} %multiply_add_fusion.1), channel_id=1, source_target_pairs={{0,32},{32,64},{64,96},{96,128},{128,160},{160,192},{192,224},{1,3... | collective-permute-start | bytes 786440 | tf_op jit(solution)/shard_map/ppermute | solution.py:13
  411.5 10.6 %collective-permute-start.6 = (f32[4,128,128]{1,2,0:T(8,128)}, f32[4,128,128]{1,2,0:T(8,128)S(1)}, u32[]{:S(2)}, u32[]{:S(2)}) collective-permute-start(f32[4,128,128]{1,2,0:T(8,128)} %multiply_add_fusion), channel_id=1, source_target_pairs={{0,32},{32,64},{64,96},{96,128},{128,160},{160,192},{192,224},{1,3... | collective-permute-start | bytes 786440 | tf_op jit(solution)/shard_map/ppermute | solution.py:13
Sparse Core Ops, SparseCore 0:
  9.9 239.4 all-gather.1
where the time goes:
time: 433 us; the launch traced here: 432 us
  waiting for transfers between devices  270 us (62%)
  matrix products  47.6 us (11%)
  other arithmetic  40 us (9%)
  starting transfers between devices  38.7 us (9%)
  local copies, waits for them, and re-layouts  22.1 us (5%)
  between operations  13.6 us (3%)
    all_gather x1, waiting for transfers between devices, body(): piece = lax.all_gather(tokens, 'zero', axis=2, tiled=True)  89.1 us
    all_to_all x1, waiting for transfers between devices, body(): lax.all_to_all(forget_weight, 'zero', split_axis=1, concat_axis=0, tiled=...  60.9 us
    ppermute x7, waiting for transfers between devices, from_behind(): lax.ppermute(value, axis, [(source, source + steps) for source in range(f...  60.3 us
    all_to_all x1, waiting for transfers between devices, body(): lax.all_to_all(q_weight, 'zero', split_axis=1, concat_axis=0, tiled=True)  58.6 us
    dot_general x3, matrix products, body(): jnp.einsum('stc,ch->sth', piece, matrix, preferred_element_type=jnp.float32)  30 us
    dot_general x4, other arithmetic, block_step(): jnp.einsum('tc,sc,tsc->ts', queries, in_gate, decays, precision=lax.Preci...  29.5 us
    ppermute x7, starting transfers between devices, from_behind(): lax.ppermute(value, axis, [(source, source + steps) for source in range(f...  15 us
    all_to_all x1, starting transfers between devices, body(): lax.all_to_all(forget_weight, 'zero', split_axis=1, concat_axis=0, tiled=...  11.6 us
  transfers between devices with their start and end apart: 11, of which 10 were waited for; matrix products, arithmetic and copies ran while one was open for 7% of the time, Pallas kernels for 0%

commit v1 on v0

v1 whole, which is shorter than its diff:
```python
import functools

import jax
import jax.numpy as jnp
import numpy as np
from jax import lax
from jax.experimental import pallas as pl
from jax.experimental.pallas import tpu as pltpu
from jax.sharding import PartitionSpec as P

MESH = pl.DeviceIdType.MESH
HEAD = 128
TILE = 128
LEVELS = (64, 32, 16, 8, 4, 2, 1)
OFFSETS = (0, 1, 7, 2, 6, 3, 5, 4)
SLOT = {offset: i for i, offset in enumerate(OFFSETS)}
X, Z = 4, 8


def coords():
    c, zi = lax.axis_index("ctx"), lax.axis_index("zero")
    return lax.rem(c, X), c // X, zi // 4, lax.rem(zi // 2, 2), lax.rem(zi, 2)


def place(x, yl, z, yh, k):
    return (yl * X + x, z * 4 + yh * 2 + k)


def wrap(value, n):
    return lax.rem(value + n, n)


def gather_kernel(tok, wq, wf, wv, proj, w_all, t_all, acc, other, local_sem, w1_s, w1_r, w2_s, w2_r, w3_s, w3_r, w4_s, w4_r,
                  y0_s, y0_r, y1_s, y1_r, z_s, z_r, z2_s, p_s, p_r):
    x, yl, z, yh, k = coords()
    seqs = t_all.shape[0]
    started = []

    def send(src, dst, ss, rs, target):
        copy = pltpu.make_async_remote_copy(src, dst, ss, rs, device_id=target, device_id_type=MESH)
        copy.start()
        started.append(copy)
        return copy

    z_next, z_prev = wrap(z + 1, Z), wrap(z - 1, Z)
    x_next, x_prev = wrap(x + 1, X), wrap(x - 1, X)
    up = place(x, yl, z_next, yh, k)
    down = place(x, yl, z_prev, yh, k)
    right = place(x_next, yl, z, yh, k)
    left = place(x_prev, yl, z, yh, k)
    far = place(x, yl, z, 1 - yh, k)
    pair = place(x, 1 - yl, z, yh, k)
    sibling = place(x, yl, z, yh, 1 - k)

    barrier = pltpu.get_barrier_semaphore()
    peers = [right, left, pair, sibling]
    for dz in range(Z):
        for dy in range(2):
            if dz or dy:
                peers.append(place(x, yl, wrap(z + dz, Z), 1 - yh if dy else yh, k))
    for peer in peers:
        pl.semaphore_signal(barrier, inc=1, device_id=peer, device_id_type=MESH)
    pl.semaphore_wait(barrier, len(peers))

    own = pltpu.make_async_copy(tok, t_all.at[:, 0, pl.ds(0, 256)], local_sem.at[0])
    own.start()
    y0 = [send(tok.at[s, pl.ds(0, 128)], t_all.at[s, 0, pl.ds(256, 128)], y0_s.at[s], y0_r.at[s], far) for s in range(seqs)]

    part = pl.multiple_of((x * 2 + yl) * 32, 32)
    w1 = {}
    locals_ = []
    for i, dz in enumerate(OFFSETS):
        for dy in range(2):
            zt, yt = wrap(z - dz, Z), 1 - yh if dy else yh
            cols = pl.multiple_of((zt * 2 + yt) * 256, 256)
            for w, ref in enumerate((wq, wf, wv)):
                src = ref.at[pl.ds(part, 32), pl.ds(cols, 256)]
                dst = w_all.at[2 * i + dy, pl.ds(part, 32), pl.ds(w * 256, 256)]
                if i == 0 and dy == 0:
                    copy = pltpu.make_async_copy(src, dst, local_sem.at[1 + w])
                    copy.start()
                    locals_.append(copy)
                else:
                    w1[2 * i + dy, w] = send(src, dst, w1_s.at[2 * i + dy, w], w1_r.at[2 * i + dy, w], place(x, yl, zt, yt, k))
    y1 = {}
    for s in range(seqs):
        y1[s, 0] = send(tok.at[s, pl.ds(128, 128)], t_all.at[s, 0, pl.ds(384, 128)], y1_s.at[s, 0], y1_r.at[s, 0], far)
    own.wait()

    zc = {}

    def ring_start(s):
        y0[s].wait_recv()
        block = t_all.at[s, 0, pl.ds(0, 384)]
        zc[s, SLOT[7]] = send(block, t_all.at[s, SLOT[7], pl.ds(0, 384)], z_s.at[s, SLOT[7]], z_r.at[s, SLOT[7]], up)
        zc[s, SLOT[1]] = send(block, t_all.at[s, SLOT[1], pl.ds(0, 384)], z_s.at[s, SLOT[1]], z_r.at[s, SLOT[1]], down)

    def ring_hop(s, h):
        for sign, target in ((-1, up), (1, down)):
            last = 4 if (sign < 0) == (s % 2 == 0) else 3
            if h > last:
                continue
            here, there = SLOT[sign * h % Z], SLOT[sign * (h + 1) % Z]
            zc[s, here].wait_recv()
            if h < last:
                zc[s, there] = send(t_all.at[s, here, pl.ds(0, 384)], t_all.at[s, there, pl.ds(0, 384)],
                                    z_s.at[s, there], z_r.at[s, there], target)
            y1[s, here] = send(t_all.at[s, here, pl.ds(128, 128)], t_all.at[s, here, pl.ds(384, 128)],
                               y1_s.at[s, here], y1_r.at[s, here], far)

    w2, w3, w4 = {}, {}, {}

    def weights_1(g):
        if g == 0:
            for copy in locals_:
                copy.wait()
        for slot in range(4 * g, 4 * g + 4):
            if slot:
                for w in range(3):
                    w1[slot, w].wait_recv()
        piece = w_all.at[pl.ds(4 * g, 4), pl.ds(part, 32)]
        w2[g] = send(piece, piece, w2_s.at[g], w2_r.at[g], pair)

    def rows_of(g, xx):
        return w_all.at[pl.ds(4 * g, 4), pl.ds(pl.multiple_of(xx * 64, 64), 64)]

    def weights_2(g):
        w2[g].wait_recv()
        piece = rows_of(g, x)
        w3[0, g] = send(piece, piece, w3_s.at[0, g], w3_r.at[0, g], right)
        w3[1, g] = send(piece, piece, w3_s.at[1, g], w3_r.at[1, g], left)

    def weights_3(g):
        w3[0, g].wait_recv()
        w3[1, g].wait_recv()
        if g % 2 == 0:
            piece = rows_of(g, x_prev)
            w4[g] = send(piece, piece, w4_s.at[g], w4_r.at[g], right)
        else:
            piece = rows_of(g, x_next)
            w4[g] = send(piece, piece, w4_s.at[g], w4_r.at[g], left)

    pc = {}

    def project(s):
        if s == 0:
            for g in range(4):
                w4[g].wait_recv()
        for i in range(Z):
            y1[s, i].wait_recv()
        lhs = jnp.concatenate([t_all[s, i, pl.ds(dy * 256, 256), :] for i in range(Z) for dy in range(2)], axis=1)
        for n in range(3):
            rhs = w_all[:, :, pl.ds(n * 256, 256)].reshape(16 * 256, 256)
            acc[s, :, pl.ds(n * 256, 256)] = jnp.dot(lhs, rhs, preferred_element_type=jnp.float32)
        theirs = pl.multiple_of((1 - k) * 128, 128)
        for n in range(3):
            pc[s, n] = send(acc.at[s, :, pl.ds(n * 256 + theirs, 128)], other.at[s, :, pl.ds(n * 128, 128)],
                            p_s.at[s, n], p_r.at[s, n], sibling)

    def collect(s):
        mine = pl.multiple_of(k * 128, 128)
        for n in range(3):
            pc[s, n].wait_recv()
            proj[s, :, pl.ds(n * 128, 128)] = acc[s, :, pl.ds(n * 256 + mine, 128)] + other[s, :, pl.ds(n * 128, 128)]

    ring_start(0)
    ring_start(1)
    weights_1(0)
    weights_1(1)
    ring_hop(0, 1)
    ring_hop(1, 1)
    weights_1(2)
    weights_1(3)
    weights_2(0)
    weights_2(1)
    ring_hop(0, 2)
    ring_hop(1, 2)
    weights_2(2)
    weights_2(3)
    ring_start(2)
    ring_hop(0, 3)
    ring_hop(1, 3)
    ring_start(3)
    weights_3(0)
    weights_3(1)
    ring_hop(0, 4)
    ring_hop(1, 4)
    ring_hop(2, 1)
    ring_hop(3, 1)
    weights_3(2)
    weights_3(3)
    ring_hop(2, 2)
    ring_hop(3, 2)
    project(0)
    ring_hop(2, 3)
    ring_hop(3, 3)
    project(1)
    ring_hop(2, 4)
    ring_hop(3, 4)
    collect(0)
    collect(1)
    project(2)
    project(3)
    collect(2)
    collect(3)
    for copy in started:
        copy.wait_send()


def gather_project(tokens, q_weight, forget_weight, value_weight):
    seqs = tokens.shape[0]
    dma = pltpu.SemaphoreType.DMA
    any_ = pl.BlockSpec(memory_space=pl.ANY)
    return pl.pallas_call(
        gather_kernel,
        out_shape=jax.ShapeDtypeStruct((seqs, 256, 384), jnp.float32),
        in_specs=[any_] * 4,
        out_specs=pl.BlockSpec(memory_space=pltpu.VMEM),
        scratch_shapes=[
            pltpu.VMEM((16, 256, 768), jnp.bfloat16),
            pltpu.VMEM((seqs, Z, 512, 256), jnp.bfloat16),
            pltpu.VMEM((seqs, 256, 768), jnp.float32),
            pltpu.VMEM((seqs, 256, 384), jnp.float32),
            dma((4,)),
            dma((16, 3)), dma((16, 3)),
            dma((4,)), dma((4,)),
            dma((2, 4)), dma((2, 4)),
            dma((4,)), dma((4,)),
            dma((seqs,)), dma((seqs,)),
            dma((seqs, Z)), dma((seqs, Z)),
            dma((seqs, Z)), dma((seqs, Z)),
            dma((1,)),
            dma((seqs, 3)), dma((seqs, 3)),
        ],
        compiler_params=pltpu.CompilerParams(collective_id=0, has_side_effects=True, vmem_limit_bytes=56 * 2**20),
        name="gather_project",
    )(tokens, q_weight, forget_weight, value_weight)


def decay_sums():
    t = np.arange(TILE)[:, None]
    r = np.arange(TILE)[None, :]
    rows = []
    for m in LEVELS:
        start = t // m * m
        upper = (t // m) % 2 == 1
        rows.append(np.where(upper, (r >= start) & (r <= t), (r > t) & (r < start + m)))
    rows.append(r <= t)
    rows.append(r > t)
    one = np.concatenate(rows, axis=0)
    return np.concatenate([one, one, one], axis=1).astype(np.float32)


def halves(value):
    high = value.astype(jnp.bfloat16)
    return high, (value - high.astype(jnp.float32)).astype(jnp.bfloat16)


def dot3(a, b, contract):
    (ah, al), (bh, bl) = a, b
    lhs = jnp.concatenate([ah, ah, al], axis=contract[0])
    rhs = jnp.concatenate([bh, bl, bh], axis=contract[1])
    return lax.dot_general(lhs, rhs, (((contract[0],), (contract[1],)), ((), ())), preferred_element_type=jnp.float32)


def log1p_unit(e):
    w = e / (2.0 + e)
    w2 = w * w
    series = jnp.full_like(w2, 1.0 / 17)
    for odd in (15, 13, 11, 9, 7, 5, 3, 1):
        series = series * w2 + 1.0 / odd
    return 2.0 * w * series


def recur_kernel(proj, bias, gain, sums, out, local_out, q_decayed, states, total, from_pair, xs_s, xs_r, ys_s, ys_r):
    x, yl, z, yh, k = coords()
    seqs = proj.shape[0]
    pair = place(x, 1 - yl, z, yh, k)
    row = [place(wrap(x + j, X), yl, z, yh, k) for j in (1, 2, 3)]
    barrier = pltpu.get_barrier_semaphore()
    for peer in row + [pair]:
        pl.semaphore_signal(barrier, inc=1, device_id=peer, device_id_type=MESH)
    pl.semaphore_wait(barrier, 4)

    def state_copy(s, j):
        piece = states.at[s, x]
        return pltpu.make_async_remote_copy(piece, piece, xs_s.at[s, j], xs_r.at[s, j], device_id=row[j], device_id_type=MESH)

    def total_copy(s):
        return pltpu.make_async_remote_copy(total.at[s], from_pair.at[s], ys_s.at[s], ys_r.at[s], device_id=pair, device_id_type=MESH)

    t = lax.broadcasted_iota(jnp.int32, (TILE, TILE), 0)
    r = lax.broadcasted_iota(jnp.int32, (TILE, TILE), 1)

    def local(s, _):
        logit = proj[s, :, pl.ds(128, 128)] + bias[...]
        e = jnp.exp(-jnp.abs(logit))
        log_forget = jnp.minimum(logit, 0.0) - log1p_unit(e)
        gate = jnp.where(logit >= 0.0, e, 1.0) / (1.0 + e)
        wide = jnp.concatenate([log_forget[:TILE], log_forget[TILE:]], axis=1)
        high = wide.astype(jnp.bfloat16)
        rest = wide - high.astype(jnp.float32)
        mid = rest.astype(jnp.bfloat16)
        low = (rest - mid.astype(jnp.float32)).astype(jnp.bfloat16)
        stacked = jnp.concatenate([high, mid, low], axis=0)

        def decays(i):
            return jnp.exp(jnp.dot(sums[pl.ds(i * TILE, TILE), :], stacked, preferred_element_type=jnp.float32))

        from_start, to_end = decays(len(LEVELS)), decays(len(LEVELS) + 1)
        queries = [proj[s, pl.ds(u * TILE, TILE), pl.ds(0, 128)] for u in range(2)]
        keys = [gate[u * TILE : (u + 1) * TILE] for u in range(2)]
        scores = [jnp.where(t == r, jnp.sum(queries[u] * keys[u], axis=1, keepdims=True), 0.0) for u in range(2)]
        for i, m in enumerate(LEVELS):
            level = decays(i)
            upper = (t // m) % 2 == 1
            differ = t ^ r
            mask = (differ >= m) & (differ < 2 * m) & (t > r)
            for u in range(2):
                item = halves(jnp.where(upper, queries[u], keys[u]) * level[:, u * 128 : (u + 1) * 128])
                scores[u] = jnp.where(mask, dot3(item, item, (1, 1)), scores[u])
        state, decay = None, None
        for u in range(2):
            lanes = slice(u * 128, (u + 1) * 128)
            values = halves(proj[s, pl.ds(u * TILE, TILE), pl.ds(256, 128)])
            own = dot3(values, halves(keys[u] * to_end[:, lanes]), (0, 0))
            own_decay = from_start[TILE - 1 : TILE, lanes]
            outputs = dot3(halves(scores[u]), values, (1, 0))
            decayed = queries[u] * from_start[:, lanes]
            if u == 0:
                state, decay = own, own_decay
            else:
                outputs = outputs + dot3(halves(decayed), halves(state), (1, 1))
                decayed = decayed * decay
                state, decay = state * own_decay + own, decay * own_decay
            local_out[s, pl.ds(u * TILE, TILE), :] = outputs
            q_decayed[s, pl.ds(u * TILE, TILE), :] = decayed
        states[s, x, pl.ds(0, 128), :] = state
        states[s, x, pl.ds(128, 8), :] = jnp.broadcast_to(decay, (8, 128))
        for j in range(3):
            state_copy(s, j).start()
        return 0

    lax.fori_loop(0, seqs, local, 0)

    def along_x(s, _):
        for j in range(3):
            state_copy(s, j).wait_recv()
        run = jnp.zeros((HEAD, HEAD), jnp.float32)
        run_decay = jnp.ones((1, HEAD), jnp.float32)
        before, before_decay = run, run_decay
        for xx in range(X):
            before = jnp.where(xx == x, run, before)
            before_decay = jnp.where(xx == x, run_decay, before_decay)
            decay = states[s, xx, pl.ds(128, 1), :]
            run = run * decay + states[s, xx, pl.ds(0, 128), :]
            run_decay = run_decay * decay
        total[s] = run
        total_copy(s).start()
        for j in range(3):
            state_copy(s, j).wait_send()
        states[s, x, pl.ds(0, 128), :] = before
        states[s, x, pl.ds(128, 8), :] = jnp.broadcast_to(before_decay, (8, 128))
        return 0

    lax.fori_loop(0, seqs, along_x, 0)

    def finish(s, _):
        total_copy(s).wait_recv()
        incoming = states[s, x, pl.ds(0, 128), :]
        earlier = from_pair[s] * states[s, x, pl.ds(128, 1), :]
        incoming = incoming + jnp.where(yl == 1, earlier, 0.0)
        outputs = local_out[s] + dot3(halves(q_decayed[s]), halves(incoming), (1, 1))
        mean_square = jnp.mean(outputs * outputs, axis=-1, keepdims=True)
        out[s] = (outputs * lax.rsqrt(mean_square + 1e-05) * gain[...]).astype(jnp.bfloat16)
        total_copy(s).wait_send()
        return 0

    lax.fori_loop(0, seqs, finish, 0)


def recur(proj, bias, gain):
    seqs = proj.shape[0]
    dma = pltpu.SemaphoreType.DMA
    vmem = pl.BlockSpec(memory_space=pltpu.VMEM)
    sums = jnp.asarray(decay_sums(), jnp.bfloat16)
    return pl.pallas_call(
        recur_kernel,
        out_shape=jax.ShapeDtypeStruct((seqs, 256, HEAD), jnp.bfloat16),
        in_specs=[vmem] * 4,
        out_specs=vmem,
        scratch_shapes=[
            pltpu.VMEM((seqs, 256, HEAD), jnp.float32),
            pltpu.VMEM((seqs, 256, HEAD), jnp.float32),
            pltpu.VMEM((seqs, X, HEAD + 8, HEAD), jnp.float32),
            pltpu.VMEM((seqs, HEAD, HEAD), jnp.float32),
            pltpu.VMEM((seqs, HEAD, HEAD), jnp.float32),
            dma((seqs, 3)), dma((seqs, 3)),
            dma((seqs,)), dma((seqs,)),
        ],
        compiler_params=pltpu.CompilerParams(collective_id=1, has_side_effects=True, vmem_limit_bytes=56 * 2**20),
        name="recur",
    )(proj, bias.reshape(1, HEAD), gain.reshape(1, HEAD), sums)


def body(tokens, q_weight, forget_weight, value_weight, forget_bias, norm_gain):
    proj = gather_project(tokens, q_weight, forget_weight, value_weight)
    return recur(proj, forget_bias, norm_gain)


def solution(mesh):
    placed = (
        P(None, "ctx", "zero"),
        P("zero", None),
        P("zero", None),
        P("zero", None),
        P("zero"),
        P("zero"),
    )
    return jax.shard_map(
        body, mesh=mesh, in_specs=placed, out_specs=P(None, "ctx", "zero"), check_vma=False
    )
```

time: 433 us -> 138 us (0.32)
  the two profiles are of different devices: /device:TPU:24 before, /device:TPU:1 now
where the time goes in v1:
time: 138 us
  Pallas kernels  137 us (99%)
  local copies, waits for them, and re-layouts  1.67 us (1%)
    pallas_call x1, Pallas kernels, gather_project(): pl.pallas_call(gather_kernel, out_shape=jax.ShapeDtypeStruct((seqs, 256,...  112 us
    pallas_call x1, Pallas kernels, recur(): pl.pallas_call(recur_kernel, out_shape=jax.ShapeDtypeStruct((seqs, 256, H...  24.2 us

profile of v1, /device:TPU:1, one launch (start us, length us, event | category | flops | bytes accessed | tf_op | source)
XLA Modules:
  0.0 138.2 jit_solution(6894260977677319181)
XLA Ops:
  0.0 112.3 %gather_project.1.proj = f32[4,256,384]{2,1,0:T(8,128)} custom-call(bf16[4,256,256]{2,1,0:T(8,128)(2,1)} %tok.1, bf16[256,4096]{1,0:T(8,128)(2,1)} %wq.1, bf16[256,4096]{1,0:T(8,128)(2,1)} %wf.1, bf16[256,4096]{1,0:T(8,128)(2,1)} %wv.1), custom_call_target="tpu_custom_call" | custom-call | tf_op jit(solution)/shard_map/gather_project/pallas_call | solution.py:214
  112.4 24.2 %recur.1 = bf16[4,256,128]{2,1,0:T(8,128)(2,1)} custom-call(f32[4,256,384]{2,1,0:T(8,128)} %gather_project.1.proj, f32[1,128]{1,0:T(1,128)} %bitcast.2, f32[1,128]{1,0:T(1,128)} %bitcast.3, bf16[1152,384]{1,0:T(8,128)(2,1)} %constant.2.clone.sums), custom_call_target="tpu_custom_call" | custom-call | tf_op jit(solution)/shard_map/recur/pallas_call | solution.py:387
  136.5 1.7 %copy.9 = bf16[4,256,128]{2,1,0:T(8,128)(2,1)} copy(bf16[4,256,128]{2,1,0:T(8,128)(2,1)} %recur.1) | data formatting | bytes 524288

commit v2 on v0

v2 whole, which is shorter than its diff:
```python
import jax
import jax.numpy as jnp
from jax import lax
from jax.experimental import pallas as pl
from jax.experimental.pallas import tpu as pltpu
from jax.sharding import PartitionSpec as P

MESH = pl.DeviceIdType.MESH
HEAD = 128
TILE = 128
LEVELS = (64, 32, 16, 8, 4, 2, 1)
OFFSETS = (1, 7, 2, 6, 0, 4, 3, 5)
SLOT = {offset: i for i, offset in enumerate(OFFSETS)}
X, Y, Z = 4, 4, 8
HEADS_HERE = 4
UNITS = ((1, 0, 256), (1, 256, 256), (2, 0, 256), (2, 256, 256), (0, 0, 256), (0, 256, 128), (0, 384, 128))
SCHEDULE = (
    ("cross_send",), ("w_send", 0), ("w_send", 1), ("share_affine",), ("sums",), ("ring", 0, 0, 0), ("ring", 1, 0, 0),
    ("a", 0, 0), ("ring", 0, 1, 0), ("b", 0, 0), ("a", 1, 0), ("ring", 1, 1, 0), ("b", 1, 0), ("b", 0, 1), ("a", 0, 1),
    ("w_send", 2), ("a", 1, 1), ("w_send", 3), ("ring", 0, 0, 1), ("b", 1, 1), ("a", 0, 2), ("b", 0, 2), ("a", 1, 2),
    ("b", 1, 2), ("ring", 1, 0, 1), ("ring", 0, 1, 1), ("a", 0, 3), ("b", 0, 3), ("ring", 1, 1, 1), ("a", 2, 0), ("b", 2, 0),
    ("a", 3, 0), ("a", 1, 3), ("b", 1, 3), ("b", 3, 0), ("ready", 0), ("ring", 0, 0, 2), ("a", 2, 1), ("w_send", 4),
    ("b", 2, 1), ("a", 3, 1), ("w_send", 5), ("ring", 1, 0, 2), ("ready", 1), ("b", 3, 1), ("ring", 0, 1, 2), ("a", 2, 2),
    ("b", 2, 2), ("a", 3, 2), ("b", 3, 2), ("ring", 1, 1, 2), ("ring", 0, 0, 3), ("a", 4, 0), ("a", 2, 3), ("b", 2, 3),
    ("b", 4, 0), ("a", 5, 0), ("b", 5, 0), ("ring", 1, 0, 3), ("a", 3, 3), ("b", 3, 3), ("a", 4, 1), ("w_send", 6),
    ("ring", 0, 1, 3), ("ready", 2), ("take_affine",), ("drain", 0), ("drain", 1), ("b", 4, 1), ("ring", 1, 1, 3),
    ("a", 5, 1), ("b", 5, 1), ("ring", 0, 0, 4), ("ring", 1, 0, 4), ("ready", 3), ("a", 6, 0), ("a", 4, 2), ("b", 4, 2),
    ("b", 6, 0), ("a", 5, 2), ("b", 5, 2), ("a", 6, 1), ("ring", 0, 1, 4), ("ring", 1, 1, 4), ("project", 0), ("project", 1),
    ("project", 2), ("a", 4, 3), ("b", 4, 3), ("b", 6, 1), ("project", 3), ("collect", 0), ("collect", 1), ("collect", 2),
    ("b", 5, 3), ("gate", 0), ("a", 6, 2), ("a", 5, 3), ("collect", 3), ("gate", 1), ("gate", 2), ("ready", 4), ("b", 6, 2),
    ("project", 4), ("gate", 3), ("state", 0), ("a", 6, 3), ("collect", 4), ("state", 1), ("ready", 5), ("project", 5),
    ("b", 6, 3), ("state", 2), ("state", 3), ("score", 0), ("ready", 6), ("collect", 5), ("project", 6), ("along_x", 0),
    ("along_x", 1), ("score", 1), ("collect", 6), ("along_x", 2), ("along_x", 3), ("score", 2), ("finish", 0), ("finish", 1),
    ("score", 3), ("finish", 2), ("finish", 3), ("drain", 2), ("drain", 3), ("drain", 4), ("drain", 5), ("drain", 6),
    ("drain_tokens",),
)


def coords():
    c, zi = lax.axis_index("ctx"), lax.axis_index("zero")
    return lax.rem(c, X), c // X, zi // 4, lax.rem(zi // 2, 2), lax.rem(zi, 2)


def place(x, yl, z, yh, k):
    return (yl * X + x, z * 4 + yh * 2 + k)


def wrap(value, n):
    return lax.rem(value + n, n)


def unit_of(weight, head):
    for u, (w, first, count) in enumerate(UNITS):
        if w == weight and first <= head * HEAD < first + count:
            return u, pl.ds(head * HEAD - first, HEAD)


def halves(value):
    high = value.astype(jnp.bfloat16)
    return high, (value - high.astype(jnp.float32)).astype(jnp.bfloat16)


def dot3(a, b, contract):
    (ah, al), (bh, bl) = a, b
    lhs = jnp.concatenate([ah, ah, al], axis=contract[0])
    rhs = jnp.concatenate([bh, bl, bh], axis=contract[1])
    return lax.dot_general(lhs, rhs, (((contract[0],), (contract[1],)), ((), ())), preferred_element_type=jnp.float32)


def log1p_unit(e):
    w = e / (2.0 + e)
    w2 = w * w
    series = jnp.full_like(w2, 1.0 / 17)
    for odd in (15, 13, 11, 9, 7, 5, 3, 1):
        series = series * w2 + 1.0 / odd
    return 2.0 * w * series


def layer_kernel(tok, wq, wf, wv, bias, gain, out, w_all, t_all, acc, other, sums, decays, gates, first_state, local_out, q_decayed,
                 states, total, from_pair, result, affine, own_s, w1_s, w1_r, ag_s, ag_r, y0_s, y0_r, z_s, z_r, p_s, p_r,
                 xs_s, xs_r, ys_s, ys_r, o_s, o_r, f_s, f_r):
    x, yl, z, yh, k = coords()
    z_next, z_prev = wrap(z + 1, Z), wrap(z - 1, Z)
    x_next, x_prev = wrap(x + 1, X), wrap(x - 1, X)
    y = yh * 2 + yl
    y_next, y_prev = wrap(y + 1, Y), wrap(y - 1, Y)
    yh_next, yl_next, yh_prev, yl_prev = y_next // 2, lax.rem(y_next, 2), y_prev // 2, lax.rem(y_prev, 2)
    z_ways = (place(x, yl, z_next, yh, k), place(x, yl, z_prev, yh, k))
    x_ways = (place(x_next, yl, z, yh, k), place(x_prev, yl, z, yh, k))
    y_ways = (place(x, yl_next, z, yh_next, k), place(x, yl_prev, z, yh_prev, k))
    row = (x_ways[0], place(wrap(x + 2, X), yl, z, yh, k), x_ways[1])
    far = place(x, yl, z, 1 - yh, k)
    pair = place(x, 1 - yl, z, yh, k)
    sibling = place(x, yl, z, yh, 1 - k)
    diagonal = place(x, yl, z, 1 - yh, 1 - k)
    mine = yh * 2 + k
    holders = [wrap(z - dz, Z) for dz in OFFSETS]
    owners = [place(x, yl, zt, yh, k) for zt in holders]
    part_a = pl.multiple_of((x * 2 + yl) * 32, 32)
    part_b = pl.multiple_of((yl * X + x) * 32, 32)

    barrier = pltpu.get_barrier_semaphore()
    peers = list(row) + list(y_ways) + [far, sibling, diagonal] + [owners[i] for i in range(Z) if i != SLOT[0]]
    for peer in peers:
        pl.semaphore_signal(barrier, inc=1, device_id=peer, device_id_type=MESH)
    pl.semaphore_wait(barrier, len(peers))

    def remote(src, dst, ss, rs, target):
        return pltpu.make_async_remote_copy(src, dst, ss, rs, device_id=target, device_id_type=MESH)


    def own_tokens(q):
        return pltpu.make_async_copy(tok.at[2 * yh + q], t_all.at[q, SLOT[0], pl.ds(pl.multiple_of(yh * 256, 256), 256)], own_s.at[q])

    def cross(q):
        return remote(tok.at[2 * (1 - yh) + q], t_all.at[q, SLOT[0], pl.ds(pl.multiple_of(yh * 256, 256), 256)],
                      y0_s.at[q], y0_r.at[q], far)

    def hops(q, way):
        return 4 if way == q else 3

    def ring_copy(q, n, way, h):
        sign = (-1, 1)[way]
        here, there = SLOT[sign * (h - 1) % Z], SLOT[sign * h % Z]
        rows = pl.ds(pl.multiple_of((1 - yh if n else yh) * 256, 256), 256)
        return remote(t_all.at[q, here, rows], t_all.at[q, there, rows], z_s.at[q, n, there], z_r.at[q, n, there], z_ways[way])

    def w1(u, i):
        w, first, count = UNITS[u]
        rows = pl.ds(part_a if i < 4 else part_b, 32)
        src = (wq, wf, wv)[w].at[rows, pl.ds(pl.multiple_of(holders[i] * 512 + first, 128), count)]
        dst = w_all.at[w, i, yh, rows, pl.ds(first, count)]
        if i == SLOT[0]:
            return pltpu.make_async_copy(src, dst, own_s.at[2 + u])
        return remote(src, dst, w1_s.at[u, i], w1_r.at[u, i], owners[i])

    def spread(u, step, way):
        w, first, count = UNITS[u]
        forward = step % 2 == 1
        base = 0 if step < 4 else 4
        slots = pl.ds(base + 2 * way, 2) if forward else pl.ds(base, 4)
        yh_from, yl_from = ((yh_prev, yl_prev), (yh_next, yl_next))[way] if forward else (yh, yl)
        x_from = (x_prev, x_next)[way] if forward else x
        if step in (0, 1):
            highs, rows, ways = pl.ds(yh_from, 1), pl.ds(pl.multiple_of((x * 2 + yl_from) * 32, 32), 32), y_ways
        elif step in (2, 3):
            highs, rows, ways = pl.ds(0, 2), pl.ds(pl.multiple_of(x_from * 64, 64), 64), x_ways
        elif step in (4, 5):
            highs, rows, ways = pl.ds(yh, 1), pl.ds(pl.multiple_of((yl * X + x_from) * 32, 32), 32), x_ways
        else:
            highs, rows, ways = pl.ds(yh_from, 1), pl.ds(pl.multiple_of(yl_from * 128, 128), 128), y_ways
        piece = w_all.at[w, slots, highs, rows, pl.ds(first, count)]
        return remote(piece, piece, ag_s.at[u, step, way], ag_r.at[u, step, way], ways[way])

    def partial(u):
        count = UNITS[u][2]
        return remote(acc.at[u, 1 - k, :, pl.ds(0, count)], other.at[u, :, pl.ds(0, count)], p_s.at[u], p_r.at[u], sibling)

    def state_copy(j, way):
        piece = states.at[j, x]
        return remote(piece, piece, xs_s.at[j, way], xs_r.at[j, way], row[way])

    def total_copy(j):
        return remote(total.at[j], from_pair.at[j], ys_s.at[j], ys_r.at[j], pair)

    def result_copy(j):
        return remote(result.at[j], out.at[mine], o_s.at[j], o_r.at[mine], place(x, yl, z, j // 2, j % 2))

    def affine_copy(n):
        piece = affine.at[mine]
        return remote(piece, piece, f_s.at[n], f_r.at[n], (sibling, far, diagonal)[n])


    def both(make, *which):
        for way in range(2):
            make(*which, way).start()

    def wait_both(make, *which):
        for way in range(2):
            make(*which, way).wait_recv()

    def cross_send():
        for q in range(2):
            cross(q).start()

    def w_send(u):
        for i in range(Z):
            w1(u, i).start()

    def ring(q, n, h):
        if h == 0:
            if n == 0:
                own_tokens(q).wait()
            else:
                cross(q).wait_recv()
        for way in range(2):
            if 0 < h <= hops(q, way):
                ring_copy(q, n, way, h).wait_recv()
            if h < hops(q, way):
                ring_copy(q, n, way, h + 1).start()

    def spread_step(half, u, n):
        if n == 0:
            for i in range(4 * half, 4 * half + 4):
                if i == SLOT[0]:
                    w1(u, i).wait()
                else:
                    w1(u, i).wait_recv()
        else:
            wait_both(spread, u, 4 * half + n - 1)
        both(spread, u, 4 * half + n)

    def ready(u):
        wait_both(spread, u, 3)
        wait_both(spread, u, 7)

    def project(u):
        w, first, count = UNITS[u]
        lhs = jnp.concatenate(
            [
                jnp.concatenate([t_all[q, i, pl.ds(high * 256, 256), :] for i in range(Z) for high in range(2)], axis=1)
                for q in range(2)
            ],
            axis=0,
        )
        rhs = w_all[w, :, :, :, pl.ds(first, count)].reshape(Z * 512, count)
        product = jnp.dot(lhs, rhs, preferred_element_type=jnp.float32)
        for q in range(2):
            acc[u, q, :, pl.ds(0, count)] = product[q * 256 : (q + 1) * 256]
        partial(u).start()

    def collect(u):
        partial(u).wait_recv()

    def summed(weight, head):
        u, cols = unit_of(weight, head)
        return acc[u, k, :, cols] + other[u, :, cols]

    t = lax.broadcasted_iota(jnp.int32, (TILE, TILE), 0)
    r = lax.broadcasted_iota(jnp.int32, (TILE, TILE), 1)
    lanes = [slice(u * TILE, (u + 1) * TILE) for u in range(2)]

    def make_sums():
        for i, m in enumerate(LEVELS + (TILE, 0)):
            if m == TILE:
                ones = jnp.where(r <= t, 1.0, 0.0)
            elif m == 0:
                ones = jnp.where(r > t, 1.0, 0.0)
            else:
                start = t // m * m
                after = jnp.where(r >= start, 1.0, 0.0) * jnp.where(r <= t, 1.0, 0.0)
                before = jnp.where(r > t, 1.0, 0.0) * jnp.where(r < start + m, 1.0, 0.0)
                ones = jnp.where((t // m) % 2 == 1, after, before)
            for j in range(3):
                sums[pl.ds(i * TILE, TILE), pl.ds(j * TILE, TILE)] = ones.astype(jnp.bfloat16)

    def gate(j):
        logit = summed(1, j) + affine[j, pl.ds(0, 1), :]
        e = jnp.exp(-jnp.abs(logit))
        log_forget = jnp.minimum(logit, 0.0) - log1p_unit(e)
        gates[j] = jnp.where(logit >= 0.0, e, 1.0) / (1.0 + e)
        wide = jnp.concatenate([log_forget[:TILE], log_forget[TILE:]], axis=1)
        high = wide.astype(jnp.bfloat16)
        rest = wide - high.astype(jnp.float32)
        mid = rest.astype(jnp.bfloat16)
        low = (rest - mid.astype(jnp.float32)).astype(jnp.bfloat16)
        stacked = jnp.concatenate([high, mid, low], axis=0)
        for i in range(len(LEVELS) + 2):
            decays[j, i] = jnp.exp(jnp.dot(sums[pl.ds(i * TILE, TILE), :], stacked, preferred_element_type=jnp.float32))

    def state(j):
        values = summed(2, j)
        own = []
        for u in range(2):
            kept = gates[j, lanes[u], :] * decays[j, len(LEVELS) + 1, :, lanes[u]]
            own.append(dot3(halves(values[lanes[u]]), halves(kept), (0, 0)))
        first_state[j] = own[0]
        own_decay = [decays[j, len(LEVELS), pl.ds(TILE - 1, 1), lanes[u]] for u in range(2)]
        states[j, x, pl.ds(0, HEAD), :] = own[0] * own_decay[1] + own[1]
        states[j, x, pl.ds(HEAD, 8), :] = jnp.broadcast_to(own_decay[0] * own_decay[1], (8, HEAD))
        for way in range(3):
            state_copy(j, way).start()

    def along_x(j):
        for way in range(3):
            state_copy(j, way).wait_recv()
        run = jnp.zeros((HEAD, HEAD), jnp.float32)
        run_decay = jnp.ones((1, HEAD), jnp.float32)
        before, before_decay = run, run_decay
        for xx in range(X):
            before = jnp.where(xx == x, run, before)
            before_decay = jnp.where(xx == x, run_decay, before_decay)
            decay = states[j, xx, pl.ds(HEAD, 1), :]
            run = run * decay + states[j, xx, pl.ds(0, HEAD), :]
            run_decay = run_decay * decay
        total[j] = run
        total_copy(j).start()
        for way in range(3):
            state_copy(j, way).wait_send()
        states[j, x, pl.ds(0, HEAD), :] = before
        states[j, x, pl.ds(HEAD, 8), :] = jnp.broadcast_to(before_decay, (8, HEAD))

    def score(j):
        all_queries, all_values = summed(0, j), summed(2, j)
        queries = [all_queries[rows] for rows in lanes]
        keys = [gates[j, rows, :] for rows in lanes]
        scores = [jnp.where(t == r, jnp.sum(queries[u] * keys[u], axis=1, keepdims=True), 0.0) for u in range(2)]
        for i, m in enumerate(LEVELS):
            upper = (t // m) % 2 == 1
            differ = t ^ r
            mask = (differ >= m) & (differ < 2 * m) & (t > r)
            for u in range(2):
                item = halves(jnp.where(upper, queries[u], keys[u]) * decays[j, i, :, lanes[u]])
                scores[u] = jnp.where(mask, dot3(item, item, (1, 1)), scores[u])
        for u in range(2):
            outputs = dot3(halves(scores[u]), halves(all_values[lanes[u]]), (1, 0))
            decayed = queries[u] * decays[j, len(LEVELS), :, lanes[u]]
            if u == 1:
                outputs = outputs + dot3(halves(decayed), halves(first_state[j]), (1, 1))
                decayed = decayed * decays[j, len(LEVELS), pl.ds(TILE - 1, 1), lanes[0]]
            local_out[j, lanes[u], :] = outputs
            q_decayed[j, lanes[u], :] = decayed

    def finish(j):
        total_copy(j).wait_recv()
        earlier = from_pair[j] * states[j, x, pl.ds(HEAD, 1), :]
        incoming = states[j, x, pl.ds(0, HEAD), :] + jnp.where(yl == 1, earlier, 0.0)
        outputs = local_out[j] + dot3(halves(q_decayed[j]), halves(incoming), (1, 1))
        mean_square = jnp.mean(outputs * outputs, axis=-1, keepdims=True)
        normed = (outputs * lax.rsqrt(mean_square + 1e-05) * affine[j, pl.ds(1, 1), :]).astype(jnp.bfloat16)
        result[j] = normed

        @pl.when(mine == j)
        def _():
            out[mine] = normed

        @pl.when(mine != j)
        def _():
            result_copy(j).start()

    def drain(u):
        for i in range(Z):
            if i != SLOT[0]:
                w1(u, i).wait_send()
        for step in range(8):
            for way in range(2):
                spread(u, step, way).wait_send()

    def drain_tokens():
        for q in range(2):
            cross(q).wait_send()
            for n in range(2):
                for way in range(2):
                    for h in range(1, hops(q, way) + 1):
                        ring_copy(q, n, way, h).wait_send()

    def share_affine():
        affine[mine] = jnp.zeros((8, HEAD), jnp.float32)
        affine[mine, pl.ds(0, 1), :] = bias[...]
        affine[mine, pl.ds(1, 1), :] = gain[...]
        for n in range(3):
            affine_copy(n).start()

    def take_affine():
        for n in range(3):
            affine_copy(n).wait()

    steps = {
        "cross_send": cross_send, "w_send": w_send, "ring": ring, "ready": ready, "project": project, "collect": collect,
        "gate": gate, "state": state, "along_x": along_x, "score": score, "finish": finish, "drain": drain, "drain_tokens": drain_tokens, "share_affine": share_affine, "take_affine": take_affine,
        "a": lambda u, n: spread_step(0, u, n), "b": lambda u, n: spread_step(1, u, n), "sums": make_sums,
    }
    for q in range(2):
        own_tokens(q).start()
    for what, *which in SCHEDULE:
        with jax.named_scope(what):
            steps[what](*which)
    for u in range(len(UNITS)):
        partial(u).wait_send()
    for j in range(HEADS_HERE):
        total_copy(j).wait_send()

        @pl.when(mine != j)
        def _():
            remote(result.at[j], out.at[j], o_s.at[j], o_r.at[j], place(x, yl, z, j // 2, j % 2)).wait()


def body(tokens, q_weight, forget_weight, value_weight, forget_bias, norm_gain):
    seqs = tokens.shape[0]
    dma = pltpu.SemaphoreType.DMA
    any_ = pl.BlockSpec(memory_space=pl.ANY)
    vmem = pl.BlockSpec(memory_space=pltpu.VMEM)
    units = len(UNITS)
    f32, bf16 = jnp.float32, jnp.bfloat16
    return pl.pallas_call(
        layer_kernel,
        out_shape=jax.ShapeDtypeStruct((seqs, 256, HEAD), bf16),
        in_specs=[any_] * 4 + [vmem] * 2,
        out_specs=vmem,
        scratch_shapes=[
            pltpu.VMEM((3, Z, 2, 256, 512), bf16),
            pltpu.VMEM((2, Z, 512, 256), bf16),
            pltpu.VMEM((units, 2, 256, 256), f32),
            pltpu.VMEM((units, 256, 256), f32),
            pltpu.VMEM(((len(LEVELS) + 2) * TILE, 3 * TILE), bf16),
            pltpu.VMEM((HEADS_HERE, len(LEVELS) + 2, TILE, 2 * TILE), f32),
            pltpu.VMEM((HEADS_HERE, 256, HEAD), f32),
            pltpu.VMEM((HEADS_HERE, HEAD, HEAD), f32),
            pltpu.VMEM((HEADS_HERE, 256, HEAD), f32),
            pltpu.VMEM((HEADS_HERE, 256, HEAD), f32),
            pltpu.VMEM((HEADS_HERE, X, HEAD + 8, HEAD), f32),
            pltpu.VMEM((HEADS_HERE, HEAD, HEAD), f32),
            pltpu.VMEM((HEADS_HERE, HEAD, HEAD), f32),
            pltpu.VMEM((HEADS_HERE, 256, HEAD), bf16),
            pltpu.VMEM((HEADS_HERE, 8, HEAD), f32),
            dma((2 + units,)),
            dma((units, Z)), dma((units, Z)),
            dma((units, 8, 2)), dma((units, 8, 2)),
            dma((2,)), dma((2,)),
            dma((2, 2, Z)), dma((2, 2, Z)),
            dma((units,)), dma((units,)),
            dma((HEADS_HERE, 3)), dma((HEADS_HERE, 3)),
            dma((HEADS_HERE,)), dma((HEADS_HERE,)),
            dma((HEADS_HERE,)), dma((HEADS_HERE,)),
            dma((3,)), dma((3,)),
        ],
        compiler_params=pltpu.CompilerParams(collective_id=0, has_side_effects=True, vmem_limit_bytes=56 * 2**20),
        name="layer",
    )(tokens, q_weight, forget_weight, value_weight, forget_bias.reshape(1, HEAD), norm_gain.reshape(1, HEAD))


def solution(mesh):
    placed = (
        P(None, "ctx", "zero"),
        P("zero", None),
        P("zero", None),
        P("zero", None),
        P("zero"),
        P("zero"),
    )
    return jax.shard_map(
        body, mesh=mesh, in_specs=placed, out_specs=P(None, "ctx", "zero"), check_vma=False
    )
```

time: 433 us -> 116 us (0.27)
  the two profiles are of different devices: /device:TPU:24 before, /device:TPU:1 now
where the time goes in v2:
time: 116 us
  Pallas kernels  114 us (98%)
  local copies, waits for them, and re-layouts  1.67 us (1%)
    pallas_call x1, Pallas kernels, body(): pl.pallas_call(layer_kernel, out_shape=jax.ShapeDtypeStruct((seqs, 256, H...  114 us

profile of v2, /device:TPU:1, one launch (start us, length us, event | category | flops | bytes accessed | tf_op | source)
XLA Modules:
  0.0 115.8 jit_solution(5432363141986045739)
XLA Ops:
  0.0 114.1 %layer.1 = bf16[4,256,128]{2,1,0:T(8,128)(2,1)} custom-call(bf16[4,256,256]{2,1,0:T(8,128)(2,1)} %tok.1, bf16[256,4096]{1,0:T(8,128)(2,1)} %wq.1, bf16[256,4096]{1,0:T(8,128)(2,1)} %wf.1, bf16[256,4096]{1,0:T(8,128)(2,1)} %wv.1, f32[1,128]{1,0:T(1,128)} %bitcast.2, f32[1,128]{1,0:T(1,128)} %bitcast.3), custom_call_target="tpu_custom_call" | custom-call | tf_op jit(solution)/shard_map/layer/pallas_call | solution.py:395
  114.1 1.7 %copy.8 = bf16[4,256,128]{2,1,0:T(8,128)(2,1)} copy(bf16[4,256,128]{2,1,0:T(8,128)(2,1)} %layer.1) | data formatting | bytes 524288

commit v3 on v2

v3 whole, which is shorter than its diff:
```python
import jax
import jax.numpy as jnp
from jax import lax
from jax.experimental import pallas as pl
from jax.experimental.pallas import tpu as pltpu
from jax.sharding import PartitionSpec as P

MESH = pl.DeviceIdType.MESH
HEAD = 128
TILE = 128
LEVELS = (64, 32, 16, 8, 4, 2, 1)
OFFSETS = (1, 7, 2, 6, 0, 4, 3, 5)
SLOT = {offset: i for i, offset in enumerate(OFFSETS)}
X, Y, Z = 4, 4, 8
HEADS_HERE = 4
UNITS = ((1, 0, 256), (1, 256, 256), (2, 0, 256), (2, 256, 256), (0, 0, 256), (0, 256, 256))
PRODUCTS = ((1, 0, 512), (2, 0, 512), (0, 0, 512))
SCHEDULE = (
    ("cross_send",), ("w_send", 0), ("w_send", 1), ("share_affine",), ("sums",), ("a", 0, 0), ("w_send", 2),
    ("ring", 0, 0, 0), ("ring", 1, 0, 0), ("ring", 0, 1, 0), ("b", 0, 0), ("a", 1, 0), ("w_send", 3), ("ring", 1, 1, 0),
    ("b", 1, 0), ("a", 0, 1), ("a", 2, 0), ("b", 0, 1), ("a", 1, 1), ("b", 2, 0), ("b", 1, 1), ("a", 0, 2), ("b", 0, 2),
    ("a", 2, 1), ("ring", 0, 0, 1), ("a", 1, 2), ("w_send", 4), ("b", 2, 1), ("b", 1, 2), ("ring", 1, 0, 1),
    ("ring", 0, 1, 1), ("a", 3, 0), ("b", 0, 3), ("a", 0, 3), ("a", 2, 2), ("w_send", 5), ("b", 3, 0), ("ring", 1, 1, 1),
    ("a", 1, 3), ("b", 1, 3), ("b", 2, 2), ("ring", 0, 0, 2), ("a", 3, 1), ("a", 4, 0), ("b", 4, 0), ("ready", 0),
    ("ring", 1, 0, 2), ("a", 2, 3), ("ring", 0, 1, 2), ("a", 5, 0), ("b", 3, 1), ("b", 5, 0), ("b", 2, 3), ("ready", 1),
    ("a", 3, 2), ("b", 4, 1), ("ring", 1, 1, 2), ("a", 4, 1), ("project", 0, 0, 5), ("a", 5, 1), ("ring", 0, 0, 3),
    ("b", 3, 2), ("ready", 2), ("take_affine",), ("b", 5, 1), ("a", 4, 2), ("ring", 1, 0, 3), ("ring", 0, 1, 3), ("a", 3, 3),
    ("a", 5, 2), ("b", 4, 2), ("ring", 1, 1, 3), ("b", 3, 3), ("b", 5, 2), ("ring", 0, 0, 4), ("ring", 1, 0, 4),
    ("ring", 0, 1, 4), ("ring", 1, 1, 4), ("project", 0, 5, 8), ("a", 4, 3), ("b", 4, 3), ("collect", 0), ("gate", 2),
    ("gate", 3), ("gate", 1), ("ready", 3), ("project", 1, 0, 5), ("project", 1, 5, 8), ("gate", 0), ("a", 5, 3),
    ("collect", 1), ("state", 2), ("b", 5, 3), ("state", 3), ("state", 1), ("state", 0), ("ready", 4), ("along_pair", 2),
    ("ready", 5), ("along_pair", 3), ("project", 2, 0, 8), ("along_pair", 1), ("along_pair", 0), ("along_x", 2),
    ("along_x", 3), ("collect", 2), ("score", 2), ("along_x", 1), ("score", 3), ("along_x", 0), ("finish", 2), ("score", 1),
    ("finish", 3), ("score", 0), ("finish", 1), ("finish", 0), ("drain",),
)


def coords():
    c, zi = lax.axis_index("ctx"), lax.axis_index("zero")
    return lax.rem(c, X), c // X, zi // 4, lax.rem(zi // 2, 2), lax.rem(zi, 2)


def place(x, yl, z, yh, k):
    return (yl * X + x, z * 4 + yh * 2 + k)


def wrap(value, n):
    return lax.rem(value + n, n)


def halves(value):
    high = value.astype(jnp.bfloat16)
    return high, (value - high.astype(jnp.float32)).astype(jnp.bfloat16)


def dot3(a, b, contract):
    (ah, al), (bh, bl) = a, b
    lhs = jnp.concatenate([ah, ah, al], axis=contract[0])
    rhs = jnp.concatenate([bh, bl, bh], axis=contract[1])
    return lax.dot_general(lhs, rhs, (((contract[0],), (contract[1],)), ((), ())), preferred_element_type=jnp.float32)


def log1p_unit(e):
    w = e / (2.0 + e)
    w2 = w * w
    series = jnp.full_like(w2, 1.0 / 17)
    for odd in (15, 13, 11, 9, 7, 5, 3, 1):
        series = series * w2 + 1.0 / odd
    return 2.0 * w * series


def layer_kernel(tok, wq, wf, wv, bias, gain, out, w_all, t_all, acc, other, sums, decays, gates, first_state, local_out, q_decayed,
                 states, total, from_pair, result, affine, own_s, w1_s, w1_r, ag_s, ag_r, y0_r, t_s, z_r, p_s, p_r,
                 xs_s, xs_r, ys_s, ys_r, o_s, o_r, f_s, f_r):
    x, yl, z, yh, k = coords()
    z_next, z_prev = wrap(z + 1, Z), wrap(z - 1, Z)
    x_next, x_prev = wrap(x + 1, X), wrap(x - 1, X)
    y = yh * 2 + yl
    y_next, y_prev = wrap(y + 1, Y), wrap(y - 1, Y)
    yh_next, yl_next, yh_prev, yl_prev = y_next // 2, lax.rem(y_next, 2), y_prev // 2, lax.rem(y_prev, 2)
    z_ways = (place(x, yl, z_next, yh, k), place(x, yl, z_prev, yh, k))
    x_ways = (place(x_next, yl, z, yh, k), place(x_prev, yl, z, yh, k))
    y_ways = (place(x, yl_next, z, yh_next, k), place(x, yl_prev, z, yh_prev, k))
    odd = lax.rem(x, 2)
    row = (place(x + 1 - 2 * odd, yl, z, yh, k), place(X - 1 - x, yl, z, yh, k))
    far = place(x, yl, z, 1 - yh, k)
    pair = place(x, 1 - yl, z, yh, k)
    sibling = place(x, yl, z, yh, 1 - k)
    diagonal = place(x, yl, z, 1 - yh, 1 - k)
    mine = yh * 2 + k
    heads = (mine, yh * 2 + 1 - k, (1 - yh) * 2 + k, (1 - yh) * 2 + 1 - k)
    owner_of = (None, sibling, far, diagonal)
    holders = [wrap(z - dz, Z) for dz in OFFSETS]
    owners = [place(x, yl, zt, yh, k) for zt in holders]
    part_a = pl.multiple_of((x * 2 + yl) * 32, 32)
    part_b = pl.multiple_of((yl * X + x) * 32, 32)

    barrier = pltpu.get_barrier_semaphore()
    peers = list(x_ways) + list(y_ways) + [far, sibling, diagonal] + [owners[i] for i in range(Z) if i != SLOT[0]]
    for peer in peers:
        pl.semaphore_signal(barrier, inc=1, device_id=peer, device_id_type=MESH)
    pl.semaphore_wait(barrier, len(peers))

    def remote(src, dst, ss, rs, target):
        return pltpu.make_async_remote_copy(src, dst, ss, rs, device_id=target, device_id_type=MESH)


    def own_tokens():
        return pltpu.make_async_copy(tok.at[pl.ds(2 * yh, 2)], t_all.at[:, SLOT[0], pl.ds(pl.multiple_of(yh * 256, 256), 256)], own_s)

    def cross(q):
        return remote(tok.at[2 * (1 - yh) + q], t_all.at[q, SLOT[0], pl.ds(pl.multiple_of(yh * 256, 256), 256)],
                      t_s, y0_r.at[q], far)

    def hops(q, way):
        return 4 if way == q else 3

    def ring_copy(q, n, way, h):
        sign = (-1, 1)[way]
        here, there = SLOT[sign * (h - 1) % Z], SLOT[sign * h % Z]
        rows = pl.ds(pl.multiple_of((1 - yh if n else yh) * 256, 256), 256)
        return remote(t_all.at[q, here, rows], t_all.at[q, there, rows], t_s, z_r.at[q, n, h - 1], z_ways[way])

    def w1(u, i):
        w, first, count = UNITS[u]
        rows = pl.ds(part_a if i < 4 else part_b, 32)
        src = (wq, wf, wv)[w].at[rows, pl.ds(pl.multiple_of(holders[i] * 512 + first, 128), count)]
        dst = w_all.at[w, i, yh, rows, pl.ds(first, count)]
        if i == SLOT[0]:
            return pltpu.make_async_copy(src, dst, w1_r.at[u, i // 4])
        return remote(src, dst, w1_s, w1_r.at[u, i // 4], owners[i])

    def spread(u, step, way):
        w, first, count = UNITS[u]
        forward = step % 2 == 1
        base = 0 if step < 4 else 4
        slots = pl.ds(base + 2 * way, 2) if forward else pl.ds(base, 4)
        yh_from, yl_from = ((yh_prev, yl_prev), (yh_next, yl_next))[way] if forward else (yh, yl)
        x_from = (x_prev, x_next)[way] if forward else x
        if step in (0, 1):
            highs, rows, ways = pl.ds(yh_from, 1), pl.ds(pl.multiple_of((x * 2 + yl_from) * 32, 32), 32), y_ways
        elif step in (2, 3):
            highs, rows, ways = pl.ds(0, 2), pl.ds(pl.multiple_of(x_from * 64, 64), 64), x_ways
        elif step in (4, 5):
            highs, rows, ways = pl.ds(yh, 1), pl.ds(pl.multiple_of((yl * X + x_from) * 32, 32), 32), x_ways
        else:
            highs, rows, ways = pl.ds(yh_from, 1), pl.ds(pl.multiple_of(yl_from * 128, 128), 128), y_ways
        piece = w_all.at[w, slots, highs, rows, pl.ds(first, count)]
        return remote(piece, piece, ag_s, ag_r.at[u, step], ways[way])

    def partial(p):
        w, first, count = PRODUCTS[p]
        cols = pl.ds(w * 512 + first, count)
        return remote(acc.at[1 - k, :, cols], other.at[:, cols], p_s, p_r.at[p], sibling)

    def state_copy(j, step):
        return remote(states.at[j, 2 * step], states.at[j, 2 * step + 1], xs_s, xs_r.at[j, step], row[step])

    def total_copy(j):
        return remote(total.at[j], from_pair.at[j], ys_s, ys_r.at[j], pair)

    def result_copy(j):
        return remote(result.at[j], out.at[mine], o_s, o_r, owner_of[j])

    def affine_copy(n):
        piece = affine.at[mine]
        return remote(piece, piece, f_s, f_r, owner_of[1 + n])

    def arrived(piece, sem):
        remote(piece, piece, t_s, sem, far).wait_recv()

    def left_here(piece, sem):
        remote(piece, piece, sem, y0_r.at[0], far).wait_send()


    def both(make, *which):
        for way in range(2):
            make(*which, way).start()

    def wait_both(u, step):
        w, first, count = UNITS[u]
        slots, highs, rows = ((8, 1, 32), (4, 1, 32), (8, 2, 64), (4, 2, 64), (8, 1, 32), (4, 1, 32), (8, 1, 128), (4, 1, 128))[step]
        arrived(w_all.at[w, pl.ds(0, slots), pl.ds(0, highs), pl.ds(0, rows), pl.ds(first, count)], ag_r.at[u, step])

    def cross_send():
        for q in range(2):
            cross(q).start()

    def w_send(u):
        for i in range(Z):
            w1(u, i).start()

    def ring(q, n, h):
        if h == 0:
            if n:
                cross(q).wait_recv()
            elif q == 0:
                own_tokens().wait()
        else:
            ways = sum(h <= hops(q, way) for way in range(2))
            arrived(t_all.at[0, 0, pl.ds(0, 256 * ways)], z_r.at[q, n, h - 1])
        for way in range(2):
            if h < hops(q, way):
                ring_copy(q, n, way, h + 1).start()

    def spread_step(half, u, n):
        if n == 0:
            w, first, count = UNITS[u]
            arrived(w_all.at[w, pl.ds(0, 4), 0, pl.ds(0, 32), pl.ds(first, count)], w1_r.at[u, half])
        else:
            wait_both(u, 4 * half + n - 1)
        both(spread, u, 4 * half + n)

    def ready(u):
        wait_both(u, 3)
        wait_both(u, 7)

    def project(p, begin, end):
        w, first, count = PRODUCTS[p]
        lhs = jnp.concatenate(
            [
                jnp.concatenate([t_all[q, i, pl.ds(high * 256, 256), :] for i in range(begin, end) for high in range(2)], axis=1)
                for q in range(2)
            ],
            axis=0,
        )
        rhs = w_all[w, pl.ds(begin, end - begin), :, :, pl.ds(first, count)].reshape((end - begin) * 512, count)
        product = jnp.dot(lhs, rhs, preferred_element_type=jnp.float32)
        cols = pl.ds(w * 512 + first, count)
        for q in range(2):
            rows = product[q * 256 : (q + 1) * 256]
            acc[q, :, cols] = acc[q, :, cols] + rows if begin else rows
        if end == Z:
            partial(p).start()

    def collect(p):
        partial(p).wait_recv()

    def summed(weight, head):
        cols = pl.ds(pl.multiple_of(weight * 512 + heads[head] * HEAD, HEAD), HEAD)
        return acc[k, :, cols] + other[:, cols]

    t = lax.broadcasted_iota(jnp.int32, (TILE, TILE), 0)
    r = lax.broadcasted_iota(jnp.int32, (TILE, TILE), 1)
    lanes = [slice(u * TILE, (u + 1) * TILE) for u in range(2)]

    def make_sums():
        for i, m in enumerate(LEVELS + (TILE, 0)):
            if m == TILE:
                ones = jnp.where(r <= t, 1.0, 0.0)
            elif m == 0:
                ones = jnp.where(r > t, 1.0, 0.0)
            else:
                start = t // m * m
                after = jnp.where(r >= start, 1.0, 0.0) * jnp.where(r <= t, 1.0, 0.0)
                before = jnp.where(r > t, 1.0, 0.0) * jnp.where(r < start + m, 1.0, 0.0)
                ones = jnp.where((t // m) % 2 == 1, after, before)
            for j in range(3):
                sums[pl.ds(i * TILE, TILE), pl.ds(j * TILE, TILE)] = ones.astype(jnp.bfloat16)

    def gate(j):
        logit = summed(1, j) + affine[heads[j], pl.ds(0, 1), :]
        e = jnp.exp(-jnp.abs(logit))
        log_forget = jnp.minimum(logit, 0.0) - log1p_unit(e)
        gates[j] = jnp.where(logit >= 0.0, e, 1.0) / (1.0 + e)
        wide = jnp.concatenate([log_forget[:TILE], log_forget[TILE:]], axis=1)
        high = wide.astype(jnp.bfloat16)
        rest = wide - high.astype(jnp.float32)
        mid = rest.astype(jnp.bfloat16)
        low = (rest - mid.astype(jnp.float32)).astype(jnp.bfloat16)
        stacked = jnp.concatenate([high, mid, low], axis=0)
        for i in range(len(LEVELS) + 2):
            decays[j, i] = jnp.exp(jnp.dot(sums[pl.ds(i * TILE, TILE), :], stacked, preferred_element_type=jnp.float32))

    def state(j):
        values = summed(2, j)
        own = []
        for u in range(2):
            kept = gates[j, lanes[u], :] * decays[j, len(LEVELS) + 1, :, lanes[u]]
            own.append(dot3(halves(values[lanes[u]]), halves(kept), (0, 0)))
        first_state[j] = own[0]
        own_decay = [decays[j, len(LEVELS), pl.ds(TILE - 1, 1), lanes[u]] for u in range(2)]
        put_state(j, 0, own[0] * own_decay[1] + own[1], own_decay[0] * own_decay[1])
        state_copy(j, 0).start()

    def put_state(j, n, value, decay):
        states[j, n, pl.ds(0, HEAD), :] = value
        states[j, n, pl.ds(HEAD, 8), :] = jnp.broadcast_to(decay, (8, HEAD))

    def get_state(j, n):
        return states[j, n, pl.ds(0, HEAD), :], states[j, n, pl.ds(HEAD, 1), :]

    def along_pair(j):
        state_copy(j, 0).wait_recv()
        (own, own_decay), (mate, mate_decay) = get_state(j, 0), get_state(j, 1)
        after = odd == 1
        joined = jnp.where(after, mate * own_decay + own, own * mate_decay + mate)
        put_state(j, 2, joined, own_decay * mate_decay)
        state_copy(j, 1).start()

    def along_x(j):
        state_copy(j, 1).wait_recv()
        (mate, mate_decay), (own, own_decay), (pairs, pairs_decay) = get_state(j, 1), get_state(j, 2), get_state(j, 3)
        second, after = x >= 2, odd == 1
        total[j] = jnp.where(second, pairs * own_decay + own, own * pairs_decay + pairs)
        total_copy(j).start()
        near, near_decay = jnp.where(after, mate, 0.0), jnp.where(after, mate_decay, 1.0)
        put_state(j, 4, near + jnp.where(second, pairs * near_decay, 0.0), jnp.where(second, pairs_decay * near_decay, near_decay))

    def score(j):
        all_queries, all_values = summed(0, j), summed(2, j)
        queries = [all_queries[rows] for rows in lanes]
        keys = [gates[j, rows, :] for rows in lanes]
        scores = [jnp.where(t == r, jnp.sum(queries[u] * keys[u], axis=1, keepdims=True), 0.0) for u in range(2)]
        for i, m in enumerate(LEVELS):
            upper = (t // m) % 2 == 1
            differ = t ^ r
            mask = (differ >= m) & (differ < 2 * m) & (t > r)
            for u in range(2):
                item = halves(jnp.where(upper, queries[u], keys[u]) * decays[j, i, :, lanes[u]])
                scores[u] = jnp.where(mask, dot3(item, item, (1, 1)), scores[u])
        for u in range(2):
            outputs = dot3(halves(scores[u]), halves(all_values[lanes[u]]), (1, 0))
            decayed = queries[u] * decays[j, len(LEVELS), :, lanes[u]]
            if u == 1:
                outputs = outputs + dot3(halves(decayed), halves(first_state[j]), (1, 1))
                decayed = decayed * decays[j, len(LEVELS), pl.ds(TILE - 1, 1), lanes[0]]
            local_out[j, lanes[u], :] = outputs
            q_decayed[j, lanes[u], :] = decayed

    def finish(j):
        total_copy(j).wait_recv()
        row_state, row_decay = get_state(j, 4)
        incoming = row_state + jnp.where(yl == 1, from_pair[j] * row_decay, 0.0)
        outputs = local_out[j] + dot3(halves(q_decayed[j]), halves(incoming), (1, 1))
        mean_square = jnp.mean(outputs * outputs, axis=-1, keepdims=True)
        normed = (outputs * lax.rsqrt(mean_square + 1e-05) * affine[heads[j], pl.ds(1, 1), :]).astype(jnp.bfloat16)
        if j == 0:
            out[mine] = normed
        else:
            result[j] = normed
            result_copy(j).start()

    def drain():
        left_here(w_all.at[:, pl.ds(0, Z - 1), 0, pl.ds(0, 32)], w1_s)
        left_here(w_all.at[:, :, :, pl.ds(0, 240)], ag_s)
        left_here(t_all.at[:, :, pl.ds(0, 480)], t_s)
        left_here(acc.at[0, :, pl.ds(0, 3 * 512)], p_s)
        left_here(states.at[:, pl.ds(0, 2)], xs_s)
        left_here(total, ys_s)
        left_here(result.at[pl.ds(0, 3)], o_s)
        left_here(affine.at[pl.ds(0, 3)], f_s)

    def share_affine():
        affine[mine] = jnp.zeros((8, HEAD), jnp.float32)
        affine[mine, pl.ds(0, 1), :] = bias[...]
        affine[mine, pl.ds(1, 1), :] = gain[...]
        for n in range(3):
            affine_copy(n).start()

    def take_affine():
        arrived(affine.at[pl.ds(0, 3)], f_r)

    steps = {
        "cross_send": cross_send, "w_send": w_send, "ring": ring, "ready": ready, "project": project, "collect": collect,
        "gate": gate, "state": state, "along_pair": along_pair, "along_x": along_x, "score": score, "finish": finish, "drain": drain, "share_affine": share_affine, "take_affine": take_affine,
        "a": lambda u, n: spread_step(0, u, n), "b": lambda u, n: spread_step(1, u, n), "sums": make_sums,
    }
    own_tokens().start()
    for what, *which in SCHEDULE:
        with jax.named_scope(what):
            steps[what](*which)
    arrived(result.at[pl.ds(0, 3)], o_r)


def body(tokens, q_weight, forget_weight, value_weight, forget_bias, norm_gain):
    seqs = tokens.shape[0]
    dma = pltpu.SemaphoreType.DMA
    any_ = pl.BlockSpec(memory_space=pl.ANY)
    vmem = pl.BlockSpec(memory_space=pltpu.VMEM)
    units = len(UNITS)
    f32, bf16 = jnp.float32, jnp.bfloat16
    return pl.pallas_call(
        layer_kernel,
        out_shape=jax.ShapeDtypeStruct((seqs, 256, HEAD), bf16),
        in_specs=[any_] * 4 + [vmem] * 2,
        out_specs=vmem,
        scratch_shapes=[
            pltpu.VMEM((3, Z, 2, 256, 512), bf16),
            pltpu.VMEM((2, Z, 512, 256), bf16),
            pltpu.VMEM((2, 256, 3 * 512), f32),
            pltpu.VMEM((256, 3 * 512), f32),
            pltpu.VMEM(((len(LEVELS) + 2) * TILE, 3 * TILE), bf16),
            pltpu.VMEM((HEADS_HERE, len(LEVELS) + 2, TILE, 2 * TILE), f32),
            pltpu.VMEM((HEADS_HERE, 256, HEAD), f32),
            pltpu.VMEM((HEADS_HERE, HEAD, HEAD), f32),
            pltpu.VMEM((HEADS_HERE, 256, HEAD), f32),
            pltpu.VMEM((HEADS_HERE, 256, HEAD), f32),
            pltpu.VMEM((HEADS_HERE, 5, HEAD + 8, HEAD), f32),
            pltpu.VMEM((HEADS_HERE, HEAD, HEAD), f32),
            pltpu.VMEM((HEADS_HERE, HEAD, HEAD), f32),
            pltpu.VMEM((HEADS_HERE, 256, HEAD), bf16),
            pltpu.VMEM((HEADS_HERE, 8, HEAD), f32),
            dma,
            dma, dma((units, 2)),
            dma, dma((units, 8)),
            dma((2,)), dma, dma((2, 2, 4)),
            dma, dma((len(PRODUCTS),)),
            dma, dma((HEADS_HERE, 2)),
            dma, dma((HEADS_HERE,)),
            dma, dma,
            dma, dma,
        ],
        compiler_params=pltpu.CompilerParams(collective_id=0, has_side_effects=True, vmem_limit_bytes=56 * 2**20),
        name="layer",
    )(tokens, q_weight, forget_weight, value_weight, forget_bias.reshape(1, HEAD), norm_gain.reshape(1, HEAD))


def solution(mesh):
    placed = (
        P(None, "ctx", "zero"),
        P("zero", None),
        P("zero", None),
        P("zero", None),
        P("zero"),
        P("zero"),
    )
    return jax.shard_map(
        body, mesh=mesh, in_specs=placed, out_specs=P(None, "ctx", "zero"), check_vma=False
    )
```

time: 116 us -> 105 us (0.905)
  Pallas kernels: 114 us -> 104 us
    pallas_call x1, Pallas kernels: 114 us -> 104 us  [body(): pl.pallas_call(layer_kernel, out_shape=jax.ShapeDtypeStruct((seqs, 256, H...]
where the time goes in v3:
time: 105 us
  Pallas kernels  104 us (99%)
  local copies, waits for them, and re-layouts  1.67 us (2%)
    pallas_call x1, Pallas kernels, body(): pl.pallas_call(layer_kernel, out_shape=jax.ShapeDtypeStruct((seqs, 256, H...  104 us

profile of v3, /device:TPU:1, one launch (start us, length us, event | category | flops | bytes accessed | tf_op | source)
XLA Modules:
  0.0 105.3 jit_solution(1641434803581830963)
XLA Ops:
  0.0 103.7 %layer.1 = bf16[4,256,128]{2,1,0:T(8,128)(2,1)} custom-call(bf16[4,256,256]{2,1,0:T(8,128)(2,1)} %tok.1, bf16[256,4096]{1,0:T(8,128)(2,1)} %wq.1, bf16[256,4096]{1,0:T(8,128)(2,1)} %wf.1, bf16[256,4096]{1,0:T(8,128)(2,1)} %wv.1, f32[1,128]{1,0:T(1,128)} %bitcast.2, f32[1,128]{1,0:T(1,128)} %bitcast.3), custom_call_target="tpu_custom_call" | custom-call | tf_op jit(solution)/shard_map/layer/pallas_call | solution.py:383
  103.7 1.7 %copy.8 = bf16[4,256,128]{2,1,0:T(8,128)(2,1)} copy(bf16[4,256,128]{2,1,0:T(8,128)(2,1)} %layer.1) | data formatting | bytes 524288

commit v4 on v3

--- a/solution.py
+++ b/solution.py
@@ -9,29 +9,33 @@
 HEAD = 128
 TILE = 128
 LEVELS = (64, 32, 16, 8, 4, 2, 1)
-OFFSETS = (1, 7, 2, 6, 0, 4, 3, 5)
+OFFSETS = (4, 3, 5, 1, 7, 2, 6, 0)
 SLOT = {offset: i for i, offset in enumerate(OFFSETS)}
 X, Y, Z = 4, 4, 8
 HEADS_HERE = 4
 UNITS = ((1, 0, 256), (1, 256, 256), (2, 0, 256), (2, 256, 256), (0, 0, 256), (0, 256, 256))
+Y_FIRST = (4, 3, 4, 3, 4, 3)
 PRODUCTS = ((1, 0, 512), (2, 0, 512), (0, 0, 512))
 SCHEDULE = (
-    ("cross_send",), ("w_send", 0), ("w_send", 1), ("share_affine",), ("sums",), ("a", 0, 0), ("w_send", 2),
-    ("ring", 0, 0, 0), ("ring", 1, 0, 0), ("ring", 0, 1, 0), ("b", 0, 0), ("a", 1, 0), ("w_send", 3), ("ring", 1, 1, 0),
-    ("b", 1, 0), ("a", 0, 1), ("a", 2, 0), ("b", 0, 1), ("a", 1, 1), ("b", 2, 0), ("b", 1, 1), ("a", 0, 2), ("b", 0, 2),
-    ("a", 2, 1), ("ring", 0, 0, 1), ("a", 1, 2), ("w_send", 4), ("b", 2, 1), ("b", 1, 2), ("ring", 1, 0, 1),
-    ("ring", 0, 1, 1), ("a", 3, 0), ("b", 0, 3), ("a", 0, 3), ("a", 2, 2), ("w_send", 5), ("b", 3, 0), ("ring", 1, 1, 1),
-    ("a", 1, 3), ("b", 1, 3), ("b", 2, 2), ("ring", 0, 0, 2), ("a", 3, 1), ("a", 4, 0), ("b", 4, 0), ("ready", 0),
-    ("ring", 1, 0, 2), ("a", 2, 3), ("ring", 0, 1, 2), ("a", 5, 0), ("b", 3, 1), ("b", 5, 0), ("b", 2, 3), ("ready", 1),
-    ("a", 3, 2), ("b", 4, 1), ("ring", 1, 1, 2), ("a", 4, 1), ("project", 0, 0, 5), ("a", 5, 1), ("ring", 0, 0, 3),
-    ("b", 3, 2), ("ready", 2), ("take_affine",), ("b", 5, 1), ("a", 4, 2), ("ring", 1, 0, 3), ("ring", 0, 1, 3), ("a", 3, 3),
-    ("a", 5, 2), ("b", 4, 2), ("ring", 1, 1, 3), ("b", 3, 3), ("b", 5, 2), ("ring", 0, 0, 4), ("ring", 1, 0, 4),
-    ("ring", 0, 1, 4), ("ring", 1, 1, 4), ("project", 0, 5, 8), ("a", 4, 3), ("b", 4, 3), ("collect", 0), ("gate", 2),
-    ("gate", 3), ("gate", 1), ("ready", 3), ("project", 1, 0, 5), ("project", 1, 5, 8), ("gate", 0), ("a", 5, 3),
-    ("collect", 1), ("state", 2), ("b", 5, 3), ("state", 3), ("state", 1), ("state", 0), ("ready", 4), ("along_pair", 2),
-    ("ready", 5), ("along_pair", 3), ("project", 2, 0, 8), ("along_pair", 1), ("along_pair", 0), ("along_x", 2),
-    ("along_x", 3), ("collect", 2), ("score", 2), ("along_x", 1), ("score", 3), ("along_x", 0), ("finish", 2), ("score", 1),
-    ("finish", 3), ("score", 0), ("finish", 1), ("finish", 0), ("drain",),
+    ("cross_send",), ("w_send", 0, 1), ("own_send", 0), ("w_send", 1, 0), ("own_send", 1), ("w_send", 0, 0),
+    ("share_affine",), ("sums",), ("b", 0, 0), ("w_send", 3, 0), ("a", 1, 0), ("w_send", 2, 1), ("w_send", 3, 1),
+    ("own_send", 3), ("a", 0, 0), ("b", 0, 1), ("w_send", 1, 1), ("w_send", 2, 0), ("a", 3, 0), ("own_step", 0),
+    ("own_step", 1), ("b", 2, 0), ("w_send", 5, 1), ("b", 0, 2), ("a", 1, 1), ("own_send", 2), ("b", 3, 0), ("own_step", 3),
+    ("b", 1, 0), ("ring", 0, 0, 0), ("ring", 0, 1, 0), ("ring", 1, 0, 0), ("ring", 1, 1, 0), ("a", 0, 1), ("b", 2, 1),
+    ("a", 2, 0), ("a", 3, 1), ("b", 5, 0), ("b", 3, 1), ("w_send", 4, 0), ("b", 1, 1), ("ring", 0, 0, 1), ("b", 5, 1),
+    ("b", 0, 3), ("b", 2, 2), ("w_send", 5, 0), ("b", 1, 2), ("ring", 0, 1, 1), ("a", 1, 2), ("own_step", 2), ("a", 0, 2),
+    ("ring", 1, 0, 1), ("a", 2, 1), ("ring", 1, 1, 1), ("a", 1, 3), ("w_send", 4, 1), ("a", 3, 2), ("a", 4, 0), ("b", 2, 3),
+    ("ring", 0, 0, 2), ("a", 5, 0), ("a", 0, 3), ("ring", 0, 1, 2), ("b", 1, 3), ("b", 3, 2), ("a", 2, 2), ("ring", 1, 0, 2),
+    ("a", 4, 1), ("a", 3, 3), ("own_send", 4), ("ring", 1, 1, 2), ("a", 5, 1), ("b", 4, 0), ("ready", 0), ("ready", 1),
+    ("project", 0, 3, 8), ("ring", 0, 0, 3), ("ring", 0, 1, 3), ("a", 2, 3), ("own_send", 5), ("b", 3, 3), ("b", 5, 2),
+    ("ring", 1, 0, 3), ("b", 4, 1), ("a", 4, 2), ("own_step", 4), ("a", 5, 2), ("own_step", 5), ("ring", 1, 1, 3),
+    ("ready", 2), ("take_affine",), ("b", 4, 2), ("ready", 3), ("project", 1, 3, 8), ("ring", 0, 0, 4), ("ring", 1, 0, 4),
+    ("ring", 0, 1, 4), ("ring", 1, 1, 4), ("project", 0, 0, 3), ("project", 1, 0, 3), ("collect", 0), ("gate", 2),
+    ("gate", 3), ("a", 4, 3), ("collect", 1), ("state", 2), ("state", 3), ("gate", 1), ("state", 1), ("b", 5, 3), ("gate", 0),
+    ("state", 0), ("levels", 2), ("levels", 3), ("a", 5, 3), ("levels", 1), ("levels", 0), ("b", 4, 3), ("along_pair", 2),
+    ("along_pair", 3), ("along_pair", 1), ("ready", 4), ("along_x", 2), ("along_pair", 0), ("ready", 5), ("along_x", 3),
+    ("project_in_turn", 2), ("along_x", 1), ("collect", 2), ("score", 2), ("along_x", 0), ("finish", 2), ("score", 3),
+    ("finish", 3), ("score", 1), ("finish", 1), ("score", 0), ("finish", 0), ("drain",),
 )
 
 
@@ -69,8 +73,8 @@
     return 2.0 * w * series
 
 
-def layer_kernel(tok, wq, wf, wv, bias, gain, out, w_all, t_all, acc, other, sums, decays, gates, first_state, local_out, q_decayed,
-                 states, total, from_pair, result, affine, own_s, w1_s, w1_r, ag_s, ag_r, y0_r, t_s, z_r, p_s, p_r,
+def layer_kernel(tok, wq, wf, wv, bias, gain, out, w_all, t_all, acc, other, sums, logs, decays, gates, first_state, local_out, q_decayed,
+                 states, total, from_pair, result, affine, own_s, wo_r, e_s, e_r, w1_s, w1_r, ag_s, ag_r, y0_r, t_s, z_r, p_s, p_r,
                  xs_s, xs_r, ys_s, ys_r, o_s, o_r, f_s, f_r):
     x, yl, z, yh, k = coords()
     z_next, z_prev = wrap(z + 1, Z), wrap(z - 1, Z)
@@ -85,6 +89,7 @@
     row = (place(x + 1 - 2 * odd, yl, z, yh, k), place(X - 1 - x, yl, z, yh, k))
     far = place(x, yl, z, 1 - yh, k)
     pair = place(x, 1 - yl, z, yh, k)
+    opposite = place(x, 1 - yl, z, 1 - yh, k)
     sibling = place(x, yl, z, yh, 1 - k)
     diagonal = place(x, yl, z, 1 - yh, 1 - k)
     mine = yh * 2 + k
@@ -121,20 +126,31 @@
         rows = pl.ds(pl.multiple_of((1 - yh if n else yh) * 256, 256), 256)
         return remote(t_all.at[q, here, rows], t_all.at[q, there, rows], t_s, z_r.at[q, n, h - 1], z_ways[way])
 
+    def source(u, z_to, rows):
+        w, first, count = UNITS[u]
+        return (wq, wf, wv)[w].at[rows, pl.ds(pl.multiple_of(z_to * 512 + first, 128), count)]
+
     def w1(u, i):
         w, first, count = UNITS[u]
-        rows = pl.ds(part_a if i < 4 else part_b, 32)
-        src = (wq, wf, wv)[w].at[rows, pl.ds(pl.multiple_of(holders[i] * 512 + first, 128), count)]
-        dst = w_all.at[w, i, yh, rows, pl.ds(first, count)]
-        if i == SLOT[0]:
-            return pltpu.make_async_copy(src, dst, w1_r.at[u, i // 4])
-        return remote(src, dst, w1_s, w1_r.at[u, i // 4], owners[i])
+        half = int(i >= Y_FIRST[u])
+        rows = pl.ds((part_a, part_b)[half], 32)
+        return remote(source(u, holders[i], rows), w_all.at[w, i, yh, rows, pl.ds(first, count)], w1_s, w1_r.at[u, half], owners[i])
+
+    def own_rows(u):
+        w, first, count = UNITS[u]
+        return pltpu.make_async_copy(source(u, z, pl.ds(0, 256)), w_all.at[w, SLOT[0], yh, :, pl.ds(first, count)], wo_r.at[u])
+
+    def other_rows(u, step):
+        w, first, count = UNITS[u]
+        half = pl.ds(pl.multiple_of((yl if step else 1 - yl) * 128, 128), 128)
+        dst = w_all.at[w, SLOT[0], 1 - yh if step else yh, half, pl.ds(first, count)]
+        return remote(dst if step else source(u, z, half), dst, e_s, e_r.at[u, step], pair if step else opposite)
 
     def spread(u, step, way):
         w, first, count = UNITS[u]
         forward = step % 2 == 1
-        base = 0 if step < 4 else 4
-        slots = pl.ds(base + 2 * way, 2) if forward else pl.ds(base, 4)
+        slots = pl.ds(0, Y_FIRST[u]) if step < 4 else pl.ds(Y_FIRST[u], Z - 1 - Y_FIRST[u])
+        cols = pl.ds(first + way * (count // 2), count // 2) if forward else pl.ds(first, count)
         yh_from, yl_from = ((yh_prev, yl_prev), (yh_next, yl_next))[way] if forward else (yh, yl)
         x_from = (x_prev, x_next)[way] if forward else x
         if step in (0, 1):
@@ -145,7 +161,7 @@
             highs, rows, ways = pl.ds(yh, 1), pl.ds(pl.multiple_of((yl * X + x_from) * 32, 32), 32), x_ways
         else:
             highs, rows, ways = pl.ds(yh_from, 1), pl.ds(pl.multiple_of(yl_from * 128, 128), 128), y_ways
-        piece = w_all.at[w, slots, highs, rows, pl.ds(first, count)]
+        piece = w_all.at[w, slots, highs, rows, cols]
         return remote(piece, piece, ag_s, ag_r.at[u, step], ways[way])
 
     def partial(p):
@@ -179,16 +195,25 @@
 
     def wait_both(u, step):
         w, first, count = UNITS[u]
-        slots, highs, rows = ((8, 1, 32), (4, 1, 32), (8, 2, 64), (4, 2, 64), (8, 1, 32), (4, 1, 32), (8, 1, 128), (4, 1, 128))[step]
-        arrived(w_all.at[w, pl.ds(0, slots), pl.ds(0, highs), pl.ds(0, rows), pl.ds(first, count)], ag_r.at[u, step])
+        slots = Y_FIRST[u] if step < 4 else Z - 1 - Y_FIRST[u]
+        rows = (32, 32, 128, 128, 32, 32, 128, 128)[step] * (1 if step % 2 else 2)
+        arrived(w_all.at[w, pl.ds(0, slots), 0, pl.ds(0, rows), pl.ds(first, count)], ag_r.at[u, step])
 
     def cross_send():
         for q in range(2):
             cross(q).start()
 
-    def w_send(u):
-        for i in range(Z):
+    def w_send(u, half):
+        for i in range(Y_FIRST[u], Z - 1) if half else range(Y_FIRST[u]):
             w1(u, i).start()
+
+    def own_send(u):
+        other_rows(u, 0).start()
+        own_rows(u).start()
+
+    def own_step(u):
+        other_rows(u, 0).wait_recv()
+        other_rows(u, 1).start()
 
     def ring(q, n, h):
         if h == 0:
@@ -206,7 +231,8 @@
     def spread_step(half, u, n):
         if n == 0:
             w, first, count = UNITS[u]
-            arrived(w_all.at[w, pl.ds(0, 4), 0, pl.ds(0, 32), pl.ds(first, count)], w1_r.at[u, half])
+            slots = Z - 1 - Y_FIRST[u] if half else Y_FIRST[u]
+            arrived(w_all.at[w, pl.ds(0, slots), 0, pl.ds(0, 32), pl.ds(first, count)], w1_r.at[u, half])
         else:
             wait_both(u, 4 * half + n - 1)
         both(spread, u, 4 * half + n)
@@ -214,6 +240,8 @@
     def ready(u):
         wait_both(u, 3)
         wait_both(u, 7)
+        own_rows(u).wait()
+        other_rows(u, 1).wait_recv()
 
     def project(p, begin, end):
         w, first, count = PRODUCTS[p]
@@ -229,9 +257,19 @@
         cols = pl.ds(w * 512 + first, count)
         for q in range(2):
             rows = product[q * 256 : (q + 1) * 256]
-            acc[q, :, cols] = acc[q, :, cols] + rows if begin else rows
-        if end == Z:
+            acc[q, :, cols] = rows if end == Z else acc[q, :, cols] + rows
+        if begin == 0:
             partial(p).start()
+
+    def project_in_turn(p):
+        w, first, count = PRODUCTS[p]
+        cols = pl.ds(w * 512 + first, count)
+        rhs = w_all[w, :, :, :, pl.ds(first, count)].reshape(Z * 512, count)
+        for q in (1 - k, k):
+            lhs = jnp.concatenate([t_all[q, i, pl.ds(high * 256, 256), :] for i in range(Z) for high in range(2)], axis=1)
+            acc[q, :, cols] = jnp.dot(lhs, rhs, preferred_element_type=jnp.float32)
+            if q is not k:
+                partial(p).start()
 
     def collect(p):
         partial(p).wait_recv()
@@ -268,9 +306,15 @@
         rest = wide - high.astype(jnp.float32)
         mid = rest.astype(jnp.bfloat16)
         low = (rest - mid.astype(jnp.float32)).astype(jnp.bfloat16)
-        stacked = jnp.concatenate([high, mid, low], axis=0)
-        for i in range(len(LEVELS) + 2):
-            decays[j, i] = jnp.exp(jnp.dot(sums[pl.ds(i * TILE, TILE), :], stacked, preferred_element_type=jnp.float32))
+        logs[j] = jnp.concatenate([high, mid, low], axis=0)
+        fill_decays(j, len(LEVELS), len(LEVELS) + 2)
+
+    def fill_decays(j, begin, end):
+        for i in range(begin, end):
+            decays[j, i] = jnp.exp(jnp.dot(sums[pl.ds(i * TILE, TILE), :], logs[j], preferred_element_type=jnp.float32))
+
+    def levels(j):
+        fill_decays(j, 0, len(LEVELS))
 
     def state(j):
         values = summed(2, j)
@@ -343,7 +387,8 @@
 
     def drain():
         left_here(w_all.at[:, pl.ds(0, Z - 1), 0, pl.ds(0, 32)], w1_s)
-        left_here(w_all.at[:, :, :, pl.ds(0, 240)], ag_s)
+        left_here(w_all.at[:, pl.ds(0, Z - 1), :, pl.ds(0, 240)], ag_s)
+        left_here(w_all.at[:, 0, 0], e_s)
         left_here(t_all.at[:, :, pl.ds(0, 480)], t_s)
         left_here(acc.at[0, :, pl.ds(0, 3 * 512)], p_s)
         left_here(states.at[:, pl.ds(0, 2)], xs_s)
@@ -362,8 +407,8 @@
         arrived(affine.at[pl.ds(0, 3)], f_r)
 
     steps = {
-        "cross_send": cross_send, "w_send": w_send, "ring": ring, "ready": ready, "project": project, "collect": collect,
-        "gate": gate, "state": state, "along_pair": along_pair, "along_x": along_x, "score": score, "finish": finish, "drain": drain, "share_affine": share_affine, "take_affine": take_affine,
+        "cross_send": cross_send, "w_send": w_send, "own_send": own_send, "own_step": own_step, "ring": ring, "ready": ready, "project": project, "project_in_turn": project_in_turn, "collect": collect,
+        "gate": gate, "levels": levels, "state": state, "along_pair": along_pair, "along_x": along_x, "score": score, "finish": finish, "drain": drain, "share_affine": share_affine, "take_affine": take_affine,
         "a": lambda u, n: spread_step(0, u, n), "b": lambda u, n: spread_step(1, u, n), "sums": make_sums,
     }
     own_tokens().start()
@@ -382,7 +427,7 @@
     f32, bf16 = jnp.float32, jnp.bfloat16
     return pl.pallas_call(
         layer_kernel,
-        out_shape=jax.ShapeDtypeStruct((seqs, 256, HEAD), bf16),
+        out_shape=pltpu.VMEM((seqs, 256, HEAD), bf16),
         in_specs=[any_] * 4 + [vmem] * 2,
         out_specs=vmem,
         scratch_shapes=[
@@ -391,6 +436,7 @@
             pltpu.VMEM((2, 256, 3 * 512), f32),
             pltpu.VMEM((256, 3 * 512), f32),
             pltpu.VMEM(((len(LEVELS) + 2) * TILE, 3 * TILE), bf16),
+            pltpu.VMEM((HEADS_HERE, 3 * TILE, 2 * TILE), bf16),
             pltpu.VMEM((HEADS_HERE, len(LEVELS) + 2, TILE, 2 * TILE), f32),
             pltpu.VMEM((HEADS_HERE, 256, HEAD), f32),
             pltpu.VMEM((HEADS_HERE, HEAD, HEAD), f32),
@@ -401,7 +447,8 @@
             pltpu.VMEM((HEADS_HERE, HEAD, HEAD), f32),
             pltpu.VMEM((HEADS_HERE, 256, HEAD), bf16),
             pltpu.VMEM((HEADS_HERE, 8, HEAD), f32),
-            dma,
+            dma, dma((units,)),
+            dma, dma((units, 2)),
             dma, dma((units, 2)),
             dma, dma((units, 8)),
             dma((2,)), dma, dma((2, 2, 4)),

time: 105 us -> 98.2 us (0.935)
  Pallas kernels: 104 us -> 97.4 us
    pallas_call x1, Pallas kernels: 104 us -> 97.4 us  [body(): pl.pallas_call(layer_kernel, out_shape=pltpu.VMEM((seqs, 256, HEAD), bf16...]
where the time goes in v4:
time: 98.2 us; the launch traced here: 98.1 us
  Pallas kernels  97.4 us (99%)
    pallas_call x1, Pallas kernels, body(): pl.pallas_call(layer_kernel, out_shape=pltpu.VMEM((seqs, 256, HEAD), bf16...  97.4 us

profile of v4, /device:TPU:1, one launch (start us, length us, event | category | flops | bytes accessed | tf_op | source)
XLA Modules:
  0.0 98.1 jit_solution(15877385668104418180)
XLA Ops:
  0.0 97.4 %layer.1 = bf16[4,256,128]{2,1,0:T(8,128)(2,1)S(1)} custom-call(bf16[4,256,256]{2,1,0:T(8,128)(2,1)} %tok.1, bf16[256,4096]{1,0:T(8,128)(2,1)} %wq.1, bf16[256,4096]{1,0:T(8,128)(2,1)} %wf.1, bf16[256,4096]{1,0:T(8,128)(2,1)} %wv.1, f32[1,128]{1,0:T(1,128)} %bitcast.2, f32[1,128]{1,0:T(1,128)} %bitcast.3), custom_call_target="tpu_custom_call" | custom-call | tf_op jit(solution)/shard_map/layer/pallas_call | solution.py:428
  97.4 0.7 copy.8

commit v5 on v4

--- a/solution.py
+++ b/solution.py
@@ -13,29 +13,31 @@
 SLOT = {offset: i for i, offset in enumerate(OFFSETS)}
 X, Y, Z = 4, 4, 8
 HEADS_HERE = 4
-UNITS = ((1, 0, 256), (1, 256, 256), (2, 0, 256), (2, 256, 256), (0, 0, 256), (0, 256, 256))
-Y_FIRST = (4, 3, 4, 3, 4, 3)
+UNITS = ((1, 0, 128), (1, 128, 128), (1, 256, 256), (2, 0, 256), (2, 256, 256), (0, 0, 256), (0, 256, 256))
+Y_FIRST = (4, 4, 4, 3, 4, 3, 3)
 PRODUCTS = ((1, 0, 512), (2, 0, 512), (0, 0, 512))
 SCHEDULE = (
-    ("cross_send",), ("w_send", 0, 1), ("own_send", 0), ("w_send", 1, 0), ("own_send", 1), ("w_send", 0, 0),
-    ("share_affine",), ("sums",), ("b", 0, 0), ("w_send", 3, 0), ("a", 1, 0), ("w_send", 2, 1), ("w_send", 3, 1),
-    ("own_send", 3), ("a", 0, 0), ("b", 0, 1), ("w_send", 1, 1), ("w_send", 2, 0), ("a", 3, 0), ("own_step", 0),
-    ("own_step", 1), ("b", 2, 0), ("w_send", 5, 1), ("b", 0, 2), ("a", 1, 1), ("own_send", 2), ("b", 3, 0), ("own_step", 3),
-    ("b", 1, 0), ("ring", 0, 0, 0), ("ring", 0, 1, 0), ("ring", 1, 0, 0), ("ring", 1, 1, 0), ("a", 0, 1), ("b", 2, 1),
-    ("a", 2, 0), ("a", 3, 1), ("b", 5, 0), ("b", 3, 1), ("w_send", 4, 0), ("b", 1, 1), ("ring", 0, 0, 1), ("b", 5, 1),
-    ("b", 0, 3), ("b", 2, 2), ("w_send", 5, 0), ("b", 1, 2), ("ring", 0, 1, 1), ("a", 1, 2), ("own_step", 2), ("a", 0, 2),
-    ("ring", 1, 0, 1), ("a", 2, 1), ("ring", 1, 1, 1), ("a", 1, 3), ("w_send", 4, 1), ("a", 3, 2), ("a", 4, 0), ("b", 2, 3),
-    ("ring", 0, 0, 2), ("a", 5, 0), ("a", 0, 3), ("ring", 0, 1, 2), ("b", 1, 3), ("b", 3, 2), ("a", 2, 2), ("ring", 1, 0, 2),
-    ("a", 4, 1), ("a", 3, 3), ("own_send", 4), ("ring", 1, 1, 2), ("a", 5, 1), ("b", 4, 0), ("ready", 0), ("ready", 1),
-    ("project", 0, 3, 8), ("ring", 0, 0, 3), ("ring", 0, 1, 3), ("a", 2, 3), ("own_send", 5), ("b", 3, 3), ("b", 5, 2),
-    ("ring", 1, 0, 3), ("b", 4, 1), ("a", 4, 2), ("own_step", 4), ("a", 5, 2), ("own_step", 5), ("ring", 1, 1, 3),
-    ("ready", 2), ("take_affine",), ("b", 4, 2), ("ready", 3), ("project", 1, 3, 8), ("ring", 0, 0, 4), ("ring", 1, 0, 4),
-    ("ring", 0, 1, 4), ("ring", 1, 1, 4), ("project", 0, 0, 3), ("project", 1, 0, 3), ("collect", 0), ("gate", 2),
-    ("gate", 3), ("a", 4, 3), ("collect", 1), ("state", 2), ("state", 3), ("gate", 1), ("state", 1), ("b", 5, 3), ("gate", 0),
-    ("state", 0), ("levels", 2), ("levels", 3), ("a", 5, 3), ("levels", 1), ("levels", 0), ("b", 4, 3), ("along_pair", 2),
-    ("along_pair", 3), ("along_pair", 1), ("ready", 4), ("along_x", 2), ("along_pair", 0), ("ready", 5), ("along_x", 3),
-    ("project_in_turn", 2), ("along_x", 1), ("collect", 2), ("score", 2), ("along_x", 0), ("finish", 2), ("score", 3),
-    ("finish", 3), ("score", 1), ("finish", 1), ("score", 0), ("finish", 0), ("drain",),
+    ("cross_send",), ("w_send", 0, 1), ("share_affine",), ("sums",), ("w_send", 6, 1), ("w_send", 0, 0), ("own_send", 0),
+    ("w_send", 1, 0), ("w_send", 3, 0), ("own_send", 5), ("b", 0, 0), ("w_send", 3, 1), ("w_send", 4, 1), ("w_send", 2, 0),
+    ("b", 6, 0), ("a", 0, 0), ("a", 1, 0), ("b", 0, 1), ("w_send", 1, 1), ("a", 3, 0), ("b", 6, 1), ("own_step", 0),
+    ("b", 3, 0), ("b", 0, 2), ("w_send", 2, 1), ("w_send", 4, 0), ("own_step", 5), ("b", 4, 0), ("a", 0, 1), ("a", 1, 1),
+    ("a", 2, 0), ("a", 3, 1), ("w_send", 6, 0), ("b", 1, 0), ("ring", 0, 0, 0), ("ring", 0, 1, 0), ("ring", 1, 0, 0),
+    ("ring", 1, 1, 0), ("b", 3, 1), ("b", 2, 0), ("w_send", 5, 0), ("b", 4, 1), ("b", 0, 3), ("a", 4, 0), ("b", 1, 1),
+    ("a", 0, 2), ("own_send", 1), ("a", 1, 2), ("own_send", 2), ("a", 6, 0), ("b", 2, 1), ("a", 2, 1), ("b", 1, 2),
+    ("ring", 0, 0, 1), ("a", 4, 1), ("own_step", 1), ("a", 0, 3), ("own_step", 2), ("ring", 0, 1, 1), ("a", 6, 1),
+    ("a", 2, 2), ("a", 1, 3), ("a", 3, 2), ("b", 2, 2), ("own_send", 4), ("ring", 1, 0, 1), ("b", 1, 3), ("ready", 0),
+    ("b", 3, 2), ("ring", 1, 1, 1), ("a", 5, 0), ("a", 2, 3), ("a", 4, 2), ("w_send", 5, 1), ("own_send", 6), ("b", 2, 3),
+    ("own_send", 3), ("b", 4, 2), ("ring", 0, 0, 2), ("own_step", 4), ("ready", 1), ("ring", 0, 1, 2), ("a", 3, 3),
+    ("ring", 1, 0, 2), ("b", 3, 3), ("a", 5, 1), ("ring", 1, 1, 2), ("b", 5, 0), ("own_step", 6), ("own_step", 3),
+    ("ready", 2), ("take_affine",), ("project", 0, 3, 8), ("a", 4, 3), ("a", 6, 2), ("ring", 0, 0, 3), ("ring", 0, 1, 3),
+    ("b", 4, 3), ("b", 6, 2), ("b", 5, 1), ("ring", 1, 0, 3), ("a", 5, 2), ("ready", 3), ("ring", 1, 1, 3), ("ready", 4),
+    ("project", 1, 3, 8), ("a", 6, 3), ("b", 5, 2), ("ring", 0, 0, 4), ("ring", 1, 0, 4), ("ring", 0, 1, 4),
+    ("ring", 1, 1, 4), ("project", 0, 0, 3), ("project", 1, 0, 3), ("b", 6, 3), ("a", 5, 3), ("collect", 0), ("gate", 2),
+    ("gate", 3), ("gate", 1), ("collect", 1), ("state", 2), ("state", 3), ("state", 1), ("gate", 0), ("state", 0),
+    ("levels", 2), ("levels", 3), ("levels", 1), ("levels", 0), ("b", 5, 3), ("along_pair", 2), ("along_pair", 3),
+    ("ready", 6), ("along_pair", 1), ("along_x", 2), ("along_pair", 0), ("ready", 5), ("along_x", 3), ("project_in_turn", 2),
+    ("along_x", 1), ("along_x", 0), ("collect", 2), ("score", 2), ("finish", 2), ("score", 3), ("finish", 3), ("score", 1),
+    ("finish", 1), ("score", 0), ("finish", 0), ("drain",),
 )
 
 
@@ -149,8 +151,13 @@
     def spread(u, step, way):
         w, first, count = UNITS[u]
         forward = step % 2 == 1
-        slots = pl.ds(0, Y_FIRST[u]) if step < 4 else pl.ds(Y_FIRST[u], Z - 1 - Y_FIRST[u])
-        cols = pl.ds(first + way * (count // 2), count // 2) if forward else pl.ds(first, count)
+        begin, end = (0, Y_FIRST[u]) if step < 4 else (Y_FIRST[u], Z - 1)
+        if forward and count > 128:
+            first, count = first + way * (count // 2), count // 2
+        elif forward:
+            middle = (begin + end + 1) // 2
+            begin, end = (middle, end) if way else (begin, middle)
+        slots, cols = pl.ds(begin, end - begin), pl.ds(first, count)
         yh_from, yl_from = ((yh_prev, yl_prev), (yh_next, yl_next))[way] if forward else (yh, yl)
         x_from = (x_prev, x_next)[way] if forward else x
         if step in (0, 1):
@@ -356,10 +363,10 @@
         queries = [all_queries[rows] for rows in lanes]
         keys = [gates[j, rows, :] for rows in lanes]
         scores = [jnp.where(t == r, jnp.sum(queries[u] * keys[u], axis=1, keepdims=True), 0.0) for u in range(2)]
+        differ = jnp.where(t > r, t ^ r, 0)
         for i, m in enumerate(LEVELS):
-            upper = (t // m) % 2 == 1
-            differ = t ^ r
-            mask = (differ >= m) & (differ < 2 * m) & (t > r)
+            upper = (t & m) != 0
+            mask = (differ >> (len(LEVELS) - 1 - i)) == 1
             for u in range(2):
                 item = halves(jnp.where(upper, queries[u], keys[u]) * decays[j, i, :, lanes[u]])
                 scores[u] = jnp.where(mask, dot3(item, item, (1, 1)), scores[u])

time: 98.2 us -> 96.8 us (0.986)
  Pallas kernels: 97.4 us -> 96 us
    pallas_call x1, Pallas kernels: 97.4 us -> 96 us  [body(): pl.pallas_call(layer_kernel, out_shape=pltpu.VMEM((seqs, 256, HEAD), bf16...]
where the time goes in v5:
time: 96.8 us; the launch traced here: 96.7 us
  Pallas kernels  96 us (99%)
    pallas_call x1, Pallas kernels, body(): pl.pallas_call(layer_kernel, out_shape=pltpu.VMEM((seqs, 256, HEAD), bf16...  96 us

profile of v5, /device:TPU:1, one launch (start us, length us, event | category | flops | bytes accessed | tf_op | source)
XLA Modules:
  0.0 96.7 jit_solution(10177184688953008255)
XLA Ops:
  0.0 96.0 %layer.1 = bf16[4,256,128]{2,1,0:T(8,128)(2,1)S(1)} custom-call(bf16[4,256,256]{2,1,0:T(8,128)(2,1)} %tok.1, bf16[256,4096]{1,0:T(8,128)(2,1)} %wq.1, bf16[256,4096]{1,0:T(8,128)(2,1)} %wf.1, bf16[256,4096]{1,0:T(8,128)(2,1)} %wv.1, f32[1,128]{1,0:T(1,128)} %bitcast.2, f32[1,128]{1,0:T(1,128)} %bitcast.3), custom_call_target="tpu_custom_call" | custom-call | tf_op jit(solution)/shard_map/layer/pallas_call | solution.py:435
  96.0 0.7 copy.8

commit v6 on v5

--- a/solution.py
+++ b/solution.py
@@ -17,7 +17,7 @@
 Y_FIRST = (4, 4, 4, 3, 4, 3, 3)
 PRODUCTS = ((1, 0, 512), (2, 0, 512), (0, 0, 512))
 SCHEDULE = (
-    ("cross_send",), ("w_send", 0, 1), ("share_affine",), ("sums",), ("w_send", 6, 1), ("w_send", 0, 0), ("own_send", 0),
+    ("cross_send",), ("w_send", 0, 1), ("share_affine",), ("w_send", 6, 1), ("w_send", 0, 0), ("own_send", 0),
     ("w_send", 1, 0), ("w_send", 3, 0), ("own_send", 5), ("b", 0, 0), ("w_send", 3, 1), ("w_send", 4, 1), ("w_send", 2, 0),
     ("b", 6, 0), ("a", 0, 0), ("a", 1, 0), ("b", 0, 1), ("w_send", 1, 1), ("a", 3, 0), ("b", 6, 1), ("own_step", 0),
     ("b", 3, 0), ("b", 0, 2), ("w_send", 2, 1), ("w_send", 4, 0), ("own_step", 5), ("b", 4, 0), ("a", 0, 1), ("a", 1, 1),
@@ -35,8 +35,8 @@
     ("ring", 1, 1, 4), ("project", 0, 0, 3), ("project", 1, 0, 3), ("b", 6, 3), ("a", 5, 3), ("collect", 0), ("gate", 2),
     ("gate", 3), ("gate", 1), ("collect", 1), ("state", 2), ("state", 3), ("state", 1), ("gate", 0), ("state", 0),
     ("levels", 2), ("levels", 3), ("levels", 1), ("levels", 0), ("b", 5, 3), ("along_pair", 2), ("along_pair", 3),
-    ("ready", 6), ("along_pair", 1), ("along_x", 2), ("along_pair", 0), ("ready", 5), ("along_x", 3), ("project_in_turn", 2),
-    ("along_x", 1), ("along_x", 0), ("collect", 2), ("score", 2), ("finish", 2), ("score", 3), ("finish", 3), ("score", 1),
+    ("along_pair", 1), ("along_x", 2), ("along_pair", 0), ("ready", 6), ("ready", 5), ("project_in_turn", 2), ("along_x", 3),
+    ("along_x", 1), ("collect", 2), ("score", 2), ("along_x", 0), ("finish", 2), ("score", 3), ("finish", 3), ("score", 1),
     ("finish", 1), ("score", 0), ("finish", 0), ("drain",),
 )
 
@@ -75,8 +75,8 @@
     return 2.0 * w * series
 
 
-def layer_kernel(tok, wq, wf, wv, bias, gain, out, w_all, t_all, acc, other, sums, logs, decays, gates, first_state, local_out, q_decayed,
-                 states, total, from_pair, result, affine, own_s, wo_r, e_s, e_r, w1_s, w1_r, ag_s, ag_r, y0_r, t_s, z_r, p_s, p_r,
+def layer_kernel(tok, wq, wf, wv, bias, gain, out, w_all, t_all, acc, other, sums, logs, decays, key_parts, gates, first_state, local_out, q_decayed,
+                 states, total, from_pair, result, affine, own_s, last_r, e_s, e_r, w1_s, w1_r, ag_s, ag_r, y0_r, t_s, z_r, p_s, p_r,
                  xs_s, xs_r, ys_s, ys_r, o_s, o_r, f_s, f_r):
     x, yl, z, yh, k = coords()
     z_next, z_prev = wrap(z + 1, Z), wrap(z - 1, Z)
@@ -106,7 +106,6 @@
     peers = list(x_ways) + list(y_ways) + [far, sibling, diagonal] + [owners[i] for i in range(Z) if i != SLOT[0]]
     for peer in peers:
         pl.semaphore_signal(barrier, inc=1, device_id=peer, device_id_type=MESH)
-    pl.semaphore_wait(barrier, len(peers))
 
     def remote(src, dst, ss, rs, target):
         return pltpu.make_async_remote_copy(src, dst, ss, rs, device_id=target, device_id_type=MESH)
@@ -140,13 +139,13 @@
 
     def own_rows(u):
         w, first, count = UNITS[u]
-        return pltpu.make_async_copy(source(u, z, pl.ds(0, 256)), w_all.at[w, SLOT[0], yh, :, pl.ds(first, count)], wo_r.at[u])
+        return pltpu.make_async_copy(source(u, z, pl.ds(0, 256)), w_all.at[w, SLOT[0], yh, :, pl.ds(first, count)], last_r.at[u])
 
     def other_rows(u, step):
         w, first, count = UNITS[u]
         half = pl.ds(pl.multiple_of((yl if step else 1 - yl) * 128, 128), 128)
         dst = w_all.at[w, SLOT[0], 1 - yh if step else yh, half, pl.ds(first, count)]
-        return remote(dst if step else source(u, z, half), dst, e_s, e_r.at[u, step], pair if step else opposite)
+        return remote(dst if step else source(u, z, half), dst, e_s, last_r.at[u] if step else e_r.at[u], pair if step else opposite)
 
     def spread(u, step, way):
         w, first, count = UNITS[u]
@@ -169,7 +168,8 @@
         else:
             highs, rows, ways = pl.ds(yh_from, 1), pl.ds(pl.multiple_of(yl_from * 128, 128), 128), y_ways
         piece = w_all.at[w, slots, highs, rows, cols]
-        return remote(piece, piece, ag_s, ag_r.at[u, step], ways[way])
+        sem = last_r.at[u] if step % 4 == 3 else ag_r.at[u, step - step // 4]
+        return remote(piece, piece, ag_s, sem, ways[way])
 
     def partial(p):
         w, first, count = PRODUCTS[p]
@@ -204,7 +204,7 @@
         w, first, count = UNITS[u]
         slots = Y_FIRST[u] if step < 4 else Z - 1 - Y_FIRST[u]
         rows = (32, 32, 128, 128, 32, 32, 128, 128)[step] * (1 if step % 2 else 2)
-        arrived(w_all.at[w, pl.ds(0, slots), 0, pl.ds(0, rows), pl.ds(first, count)], ag_r.at[u, step])
+        arrived(w_all.at[w, pl.ds(0, slots), 0, pl.ds(0, rows), pl.ds(first, count)], ag_r.at[u, step - step // 4])
 
     def cross_send():
         for q in range(2):
@@ -245,10 +245,8 @@
         both(spread, u, 4 * half + n)
 
     def ready(u):
-        wait_both(u, 3)
-        wait_both(u, 7)
-        own_rows(u).wait()
-        other_rows(u, 1).wait_recv()
+        w, first, count = UNITS[u]
+        arrived(w_all.at[w, pl.ds(0, 5), 0, :, pl.ds(first, count)], last_r.at[u])
 
     def project(p, begin, end):
         w, first, count = PRODUCTS[p]
@@ -322,6 +320,10 @@
 
     def levels(j):
         fill_decays(j, 0, len(LEVELS))
+        for i in range(len(LEVELS)):
+            for u in range(2):
+                high, low = halves(gates[j, lanes[u], :] * decays[j, i, :, lanes[u]])
+                key_parts[j, i, u] = jnp.concatenate([high, low], axis=0)
 
     def state(j):
         values = summed(2, j)
@@ -365,11 +367,23 @@
         scores = [jnp.where(t == r, jnp.sum(queries[u] * keys[u], axis=1, keepdims=True), 0.0) for u in range(2)]
         differ = jnp.where(t > r, t ^ r, 0)
         for i, m in enumerate(LEVELS):
-            upper = (t & m) != 0
+            picked = [slice(n + m, n + 2 * m) for n in range(0, TILE, 2 * m)] if m >= 8 else [slice(0, TILE)]
             mask = (differ >> (len(LEVELS) - 1 - i)) == 1
             for u in range(2):
-                item = halves(jnp.where(upper, queries[u], keys[u]) * decays[j, i, :, lanes[u]])
-                scores[u] = jnp.where(mask, dot3(item, item, (1, 1)), scores[u])
+                level = decays[j, i, :, lanes[u]]
+                high, low = halves(jnp.concatenate([queries[u][rows] * level[rows] for rows in picked], axis=0))
+                both_parts = lax.dot_general(jnp.concatenate([high, low], axis=0), key_parts[j, i, u], (((1,), (1,)), ((), ())),
+                                             preferred_element_type=jnp.float32)
+                count = high.shape[0]
+                product = both_parts[:count, :TILE] + (both_parts[:count, TILE:] + both_parts[count:, :TILE])
+                pieces, begin = [], 0
+                for n, rows in enumerate(picked):
+                    size = rows.stop - rows.start
+                    if m >= 8:
+                        pieces.append(scores[u][rows.start - m : rows.start])
+                    pieces.append(jnp.where(mask[rows], product[begin : begin + size], scores[u][rows]))
+                    begin += size
+                scores[u] = jnp.concatenate(pieces, axis=0)
         for u in range(2):
             outputs = dot3(halves(scores[u]), halves(all_values[lanes[u]]), (1, 0))
             decayed = queries[u] * decays[j, len(LEVELS), :, lanes[u]]
@@ -403,10 +417,12 @@
         left_here(result.at[pl.ds(0, 3)], o_s)
         left_here(affine.at[pl.ds(0, 3)], f_s)
 
-    def share_affine():
+    def put_affine():
         affine[mine] = jnp.zeros((8, HEAD), jnp.float32)
         affine[mine, pl.ds(0, 1), :] = bias[...]
         affine[mine, pl.ds(1, 1), :] = gain[...]
+
+    def share_affine():
         for n in range(3):
             affine_copy(n).start()
 
@@ -416,9 +432,12 @@
     steps = {
         "cross_send": cross_send, "w_send": w_send, "own_send": own_send, "own_step": own_step, "ring": ring, "ready": ready, "project": project, "project_in_turn": project_in_turn, "collect": collect,
         "gate": gate, "levels": levels, "state": state, "along_pair": along_pair, "along_x": along_x, "score": score, "finish": finish, "drain": drain, "share_affine": share_affine, "take_affine": take_affine,
-        "a": lambda u, n: spread_step(0, u, n), "b": lambda u, n: spread_step(1, u, n), "sums": make_sums,
+        "a": lambda u, n: spread_step(0, u, n), "b": lambda u, n: spread_step(1, u, n),
     }
     own_tokens().start()
+    make_sums()
+    put_affine()
+    pl.semaphore_wait(barrier, len(peers))
     for what, *which in SCHEDULE:
         with jax.named_scope(what):
             steps[what](*which)
@@ -445,6 +464,7 @@
             pltpu.VMEM(((len(LEVELS) + 2) * TILE, 3 * TILE), bf16),
             pltpu.VMEM((HEADS_HERE, 3 * TILE, 2 * TILE), bf16),
             pltpu.VMEM((HEADS_HERE, len(LEVELS) + 2, TILE, 2 * TILE), f32),
+            pltpu.VMEM((HEADS_HERE, len(LEVELS), 2, 2 * TILE, TILE), bf16),
             pltpu.VMEM((HEADS_HERE, 256, HEAD), f32),
             pltpu.VMEM((HEADS_HERE, HEAD, HEAD), f32),
             pltpu.VMEM((HEADS_HERE, 256, HEAD), f32),
@@ -455,9 +475,9 @@
             pltpu.VMEM((HEADS_HERE, 256, HEAD), bf16),
             pltpu.VMEM((HEADS_HERE, 8, HEAD), f32),
             dma, dma((units,)),
+            dma, dma((units,)),
             dma, dma((units, 2)),
-            dma, dma((units, 2)),
-            dma, dma((units, 8)),
+            dma, dma((units, 6)),
             dma((2,)), dma, dma((2, 2, 4)),
             dma, dma((len(PRODUCTS),)),
             dma, dma((HEADS_HERE, 2)),

time: 96.8 us -> 96.4 us (level)
  no operation moved by 1% of the time
where the time goes in v6:
time: 96.4 us
  Pallas kernels  95.6 us (99%)
    pallas_call x1, Pallas kernels, body(): pl.pallas_call(layer_kernel, out_shape=pltpu.VMEM((seqs, 256, HEAD), bf16...  95.6 us

profile of v6, /device:TPU:1, one launch (start us, length us, event | category | flops | bytes accessed | tf_op | source)
XLA Modules:
  0.0 96.4 jit_solution(3315355075921222867)
XLA Ops:
  0.0 95.6 %layer.1 = bf16[4,256,128]{2,1,0:T(8,128)(2,1)S(1)} custom-call(bf16[4,256,256]{2,1,0:T(8,128)(2,1)} %tok.1, bf16[256,4096]{1,0:T(8,128)(2,1)} %wq.1, bf16[256,4096]{1,0:T(8,128)(2,1)} %wf.1, bf16[256,4096]{1,0:T(8,128)(2,1)} %wv.1, f32[1,128]{1,0:T(1,128)} %bitcast.2, f32[1,128]{1,0:T(1,128)} %bitcast.3), custom_call_target="tpu_custom_call" | custom-call | tf_op jit(solution)/shard_map/layer/pallas_call | solution.py:454
  95.7 0.7 copy.8
